TPU v7x, 32 devices: a whole 2x2x4 slice. The times are simulated.
32 devices in a mesh: fsdp: 8 (over y, x, core), tensor: 4 (over z).
Axes of the slice: x: 2, y: 2, z: 4, core: 2. Of those that a mesh axis runs over, the one named last changes fastest.
Arguments:
- states: bfloat16 [4608, 2048], P('fsdp'), may hold values from -6 to 6
- segment_ids: int32 [4608], P('fsdp'), may hold values from 0 to 143, as said below
- ln1_gain: bfloat16 [2, 2048], P(None, 'fsdp'), may hold values from 0.5 to 1.5
- ln1_bias: bfloat16 [2, 2048], P(None, 'fsdp'), may hold values from -4 to 4
- qkv_weight: bfloat16 [2, 2048, 3, 2048], P(None, 'fsdp', None, 'tensor'), may hold values from -0.125 to 0.125
- qkv_bias: bfloat16 [2, 3, 32, 64], P(None, None, 'tensor', 'fsdp'), may hold values from -4 to 4
- out_weight: bfloat16 [2, 2048, 2048], P(None, 'tensor', 'fsdp'), may hold values from -0.375 to 0.375
- ln2_gain: bfloat16 [2, 2048], P(None, 'fsdp'), may hold values from 0.5 to 1.5
- ln2_bias: bfloat16 [2, 2048], P(None, 'fsdp'), may hold values from -4 to 4
- gate_up_weight: bfloat16 [2, 2048, 2, 5632], P(None, 'fsdp', None, 'tensor'), may hold values from -0.125 to 0.125
- down_weight: bfloat16 [2, 5632, 2048], P(None, 'tensor', 'fsdp'), may hold values from -0.109375 to 0.109375
- cotangent: bfloat16 [4608, 2048], P('fsdp'), may hold values from -6 to 6
Outputs:
- out_states: bfloat16 [4608, 2048], P('fsdp')
- grad_states: float32 [4608, 2048], P('fsdp')
- grad_ln1_gain: float32 [2, 2048], P(None, 'fsdp')
- grad_ln1_bias: float32 [2, 2048], P(None, 'fsdp')
- grad_qkv_weight: float32 [2, 2048, 3, 2048], P(None, 'fsdp', None, 'tensor')
- grad_qkv_bias: float32 [2, 3, 32, 64], P(None, None, 'tensor', 'fsdp')
- grad_out_weight: float32 [2, 2048, 2048], P(None, 'tensor', 'fsdp')
- grad_ln2_gain: float32 [2, 2048], P(None, 'fsdp')
- grad_ln2_bias: float32 [2, 2048], P(None, 'fsdp')
- grad_gate_up: float32 [2, 2048, 2, 5632], P(None, 'fsdp', None, 'tensor')
- grad_down: float32 [2, 5632, 2048], P(None, 'tensor', 'fsdp')
Inputs may be any that keep to these rules, and one draw needn't show every extreme that they name: `segment_ids`: each device's block of 576 tokens holds whole sequences numbered 0, 1, 2, ... in order from the block's start; every sequence starts at a place within its block that is a multiple of 4; some block holds one sequence of all 576 tokens.
All inputs are finite; a program needn't handle non-finite values.
Results may differ from a plain program's by a relative error of at most 0.03.
Values may be sent and summed in bfloat16 or wider, within the bound.
A program may use at most 256 MiB of HBM per device.

v0:
```python
import math

import jax
import jax.numpy as jnp
from jax import lax
from jax.sharding import PartitionSpec as P

HEAD_DIM = 64
ROT_DIM = 16
LAYERS = 2


norm_epsilon = 1e-05
rotary_base = 10000.0


def layer_norm_pieces(values):
    average = jnp.mean(values, axis=-1, keepdims=True)
    centred = values - average
    spread = jnp.mean(centred * centred, axis=-1, keepdims=True)
    reciprocal_deviation = lax.rsqrt(spread + norm_epsilon)
    return (centred * reciprocal_deviation, reciprocal_deviation)


def layer_norm_backward(normalized_gradient, standardized_rows, reciprocal_deviation, norm_scale):
    centered_scaled_gradient = normalized_gradient * norm_scale
    norm_scale_gradient = jnp.sum(normalized_gradient * standardized_rows, axis=0)
    bias_grad = jnp.sum(normalized_gradient, axis=0)
    d_input = reciprocal_deviation * (
        centered_scaled_gradient
        - jnp.mean(centered_scaled_gradient, axis=-1, keepdims=True)
        - standardized_rows
        * jnp.mean(centered_scaled_gradient * standardized_rows, axis=-1, keepdims=True)
    )
    return (d_input, norm_scale_gradient, bias_grad)


def rotate(values, cosine, sine):
    half = ROT_DIM // 2
    first = values[..., :half]
    second = values[..., half:ROT_DIM]
    return jnp.concatenate(
        [first * cosine - second * sine, second * cosine + first * sine, values[..., ROT_DIM:]],
        axis=-1,
    )


def rotate_back(values, cosine, sine):
    half = ROT_DIM // 2
    first = values[..., :half]
    second = values[..., half:ROT_DIM]
    return jnp.concatenate(
        [first * cosine + second * sine, second * cosine - first * sine, values[..., ROT_DIM:]],
        axis=-1,
    )


def fetch_forward(
    first_norm_scale,
    first_norm_bias,
    qkv_w,
    qkv_b,
    out_w,
    second_norm_scale,
    second_norm_bias,
    gate_up_w,
    down_w,
):
    return (
        lax.all_gather(first_norm_scale, "fsdp", axis=0, tiled=True),
        lax.all_gather(first_norm_bias, "fsdp", axis=0, tiled=True),
        lax.all_gather(qkv_w, "fsdp", axis=0, tiled=True),
        lax.all_gather(qkv_b, "fsdp", axis=2, tiled=True),
        lax.all_gather(out_w, "fsdp", axis=1, tiled=True),
        lax.all_gather(second_norm_scale, "fsdp", axis=0, tiled=True),
        lax.all_gather(second_norm_bias, "fsdp", axis=0, tiled=True),
        lax.all_gather(gate_up_w, "fsdp", axis=0, tiled=True),
        lax.all_gather(down_w, "fsdp", axis=1, tiled=True),
    )


def fetch_backward(
    first_norm_scale,
    first_norm_bias,
    qkv_w,
    qkv_b,
    out_w,
    second_norm_scale,
    second_norm_bias,
    gate_up_w,
    down_w,
):
    return (
        lax.all_gather(first_norm_scale, "fsdp", axis=0, tiled=True),
        lax.all_gather(first_norm_bias, "fsdp", axis=0, tiled=True),
        lax.all_gather(qkv_w, "fsdp", axis=0, tiled=True),
        lax.all_gather(qkv_b, "fsdp", axis=2, tiled=True),
        lax.all_gather(out_w, "fsdp", axis=1, tiled=True),
        lax.all_gather(second_norm_scale, "fsdp", axis=0, tiled=True),
        lax.all_gather(second_norm_bias, "fsdp", axis=0, tiled=True),
        lax.all_gather(gate_up_w, "fsdp", axis=0, tiled=True),
        lax.all_gather(down_w, "fsdp", axis=1, tiled=True),
    )


def attention_scores(query_rows, key_rows, allowed):
    scores = jnp.einsum(
        "qhd,khd->hqk", query_rows, key_rows, preferred_element_type=jnp.float32
    ) * (1.0 / math.sqrt(HEAD_DIM))
    return jnp.where(allowed[None], scores, -1e30)


def forward_layer(residual_state, weights, cosine, sine, allowed):
    (
        first_norm_scale,
        first_norm_bias,
        qkv_w,
        qkv_b,
        out_w,
        second_norm_scale,
        second_norm_bias,
        gate_up_w,
        down_w,
    ) = weights
    width = residual_state.shape[1]
    local = qkv_w.shape[2]
    ff_local = gate_up_w.shape[2]
    first_standardized_rows, first_reciprocal_deviation = layer_norm_pieces(residual_state)
    normalized_rows = (
        first_standardized_rows * first_norm_scale.astype(jnp.float32)
        + first_norm_bias.astype(jnp.float32)
    ).astype(jnp.bfloat16)
    rows = normalized_rows.shape[0]
    mixed = jnp.dot(
        normalized_rows, qkv_w.reshape(width, 3 * local), preferred_element_type=jnp.float32
    ).reshape(rows, 3, local)
    mixed = mixed + qkv_b.reshape(3, local).astype(jnp.float32)[None]
    heads = mixed.reshape(rows, 3, local // HEAD_DIM, HEAD_DIM)
    query_rows = rotate(heads[:, 0], cosine, sine).astype(jnp.bfloat16)
    key_rows = rotate(heads[:, 1], cosine, sine).astype(jnp.bfloat16)
    value_rows = heads[:, 2].astype(jnp.bfloat16)
    scores = attention_scores(query_rows, key_rows, allowed)
    row_top = jnp.max(scores, axis=-1, keepdims=True)
    expd = jnp.exp(scores - row_top)
    row_total = jnp.sum(expd, axis=-1, keepdims=True)
    weights_low = (expd / row_total).astype(jnp.bfloat16)
    log_total = row_top + jnp.log(row_total)
    attended = (
        jnp.einsum("hqk,khd->qhd", weights_low, value_rows, preferred_element_type=jnp.float32)
        .reshape(rows, local)
        .astype(jnp.bfloat16)
    )
    attn_part = jnp.dot(attended, out_w, preferred_element_type=jnp.float32)
    residual_between = residual_state + lax.psum(attn_part.astype(jnp.bfloat16), "tensor").astype(
        jnp.float32
    )
    second_standardized_rows, second_reciprocal_deviation = layer_norm_pieces(residual_between)
    second_normalized_rows = (
        second_standardized_rows * second_norm_scale.astype(jnp.float32)
        + second_norm_bias.astype(jnp.float32)
    ).astype(jnp.bfloat16)
    gate_up = jnp.dot(
        second_normalized_rows,
        gate_up_w.reshape(width, 2 * ff_local),
        preferred_element_type=jnp.float32,
    ).reshape(rows, 2, ff_local)
    hidden = (jax.nn.silu(gate_up[:, 0]) * gate_up[:, 1]).astype(jnp.bfloat16)
    ff_part = jnp.dot(hidden, down_w, preferred_element_type=jnp.float32)
    result = residual_between + lax.psum(ff_part.astype(jnp.bfloat16), "tensor").astype(jnp.float32)
    saved = (
        first_standardized_rows,
        first_reciprocal_deviation,
        normalized_rows,
        query_rows,
        key_rows,
        value_rows,
        log_total,
        attended,
        second_standardized_rows,
        second_reciprocal_deviation,
        second_normalized_rows,
        gate_up,
        hidden,
    )
    return (result, saved)


def backward_layer(grad, weights, saved, cosine, sine, allowed):
    (
        first_norm_scale,
        first_norm_bias,
        qkv_w,
        qkv_b,
        out_w,
        second_norm_scale,
        second_norm_bias,
        gate_up_w,
        down_w,
    ) = weights
    (
        first_standardized_rows,
        first_reciprocal_deviation,
        normalized_rows,
        query_rows,
        key_rows,
        value_rows,
        log_total,
        attended,
        second_standardized_rows,
        second_reciprocal_deviation,
        second_normalized_rows,
        gate_up,
        hidden,
    ) = saved
    width = grad.shape[1]
    local = qkv_w.shape[2]
    ff_local = gate_up_w.shape[2]
    down_in = grad.astype(jnp.bfloat16)
    rows = down_in.shape[0]
    g_down = jnp.einsum("tf,td->fd", hidden, down_in, preferred_element_type=jnp.float32)
    d_hidden = jnp.einsum("td,fd->tf", down_in, down_w, preferred_element_type=jnp.float32)
    gate_part = gate_up[:, 0]
    up_part = gate_up[:, 1]
    sigma = jax.nn.sigmoid(gate_part)
    d_gate = d_hidden * up_part * sigma * (1.0 + gate_part * (1.0 - sigma))
    d_up = d_hidden * gate_part * sigma
    d_gate_up = jnp.stack([d_gate, d_up], axis=1).astype(jnp.bfloat16)
    g_gate_up = jnp.einsum(
        "td,tcf->dcf", second_normalized_rows, d_gate_up, preferred_element_type=jnp.float32
    )
    ff_back = jnp.einsum(
        "te,de->td",
        d_gate_up.reshape(rows, 2 * ff_local),
        gate_up_w.reshape(width, 2 * ff_local),
        preferred_element_type=jnp.float32,
    )
    second_normalized_gradient = lax.psum(ff_back.astype(jnp.bfloat16), "tensor").astype(
        jnp.float32
    )
    d_mid_norm, g_gain_two, g_bias_two = layer_norm_backward(
        second_normalized_gradient,
        second_standardized_rows,
        second_reciprocal_deviation,
        second_norm_scale.astype(jnp.float32),
    )
    d_middle = grad + d_mid_norm
    mid_in = d_middle.astype(jnp.bfloat16)
    g_out = jnp.einsum("te,td->ed", attended, mid_in, preferred_element_type=jnp.float32)
    d_attended = (
        jnp.einsum("td,ed->te", mid_in, out_w, preferred_element_type=jnp.float32)
        .reshape(rows, local // HEAD_DIM, HEAD_DIM)
        .astype(jnp.bfloat16)
    )
    scores = attention_scores(query_rows, key_rows, allowed)
    probs_full = jnp.exp(scores - log_total)
    probs_low = probs_full.astype(jnp.bfloat16)
    d_value = jnp.einsum("hqk,qhd->khd", probs_low, d_attended, preferred_element_type=jnp.float32)
    d_probs = jnp.einsum("qhd,khd->hqk", d_attended, value_rows, preferred_element_type=jnp.float32)
    d_scores = (
        probs_full * (d_probs - jnp.sum(probs_full * d_probs, axis=-1, keepdims=True))
    ).astype(jnp.bfloat16)
    scale_factor = 1.0 / math.sqrt(HEAD_DIM)
    d_query = (
        jnp.einsum("hqk,khd->qhd", d_scores, key_rows, preferred_element_type=jnp.float32)
        * scale_factor
    )
    d_key = (
        jnp.einsum("hqk,qhd->khd", d_scores, query_rows, preferred_element_type=jnp.float32)
        * scale_factor
    )
    d_mixed = jnp.stack(
        [rotate_back(d_query, cosine, sine), rotate_back(d_key, cosine, sine), d_value], axis=1
    )
    d_mixed = d_mixed.reshape(rows, 3 * local).astype(jnp.bfloat16)
    g_qkv_b = jnp.sum(d_mixed, axis=0, dtype=jnp.float32).reshape(3, local // HEAD_DIM, HEAD_DIM)
    g_qkv_w = jnp.einsum(
        "td,te->de", normalized_rows, d_mixed, preferred_element_type=jnp.float32
    ).reshape(width, 3, local)
    attn_back = jnp.einsum(
        "te,de->td", d_mixed, qkv_w.reshape(width, 3 * local), preferred_element_type=jnp.float32
    )
    first_normalized_gradient = lax.psum(attn_back.astype(jnp.bfloat16), "tensor").astype(
        jnp.float32
    )
    d_in_norm, g_gain_one, g_bias_one = layer_norm_backward(
        first_normalized_gradient,
        first_standardized_rows,
        first_reciprocal_deviation,
        first_norm_scale.astype(jnp.float32),
    )
    shares = (
        lax.psum_scatter(
            g_gain_one.astype(jnp.bfloat16), "fsdp", scatter_dimension=0, tiled=True
        ).astype(jnp.float32),
        lax.psum_scatter(
            g_bias_one.astype(jnp.bfloat16), "fsdp", scatter_dimension=0, tiled=True
        ).astype(jnp.float32),
        lax.psum_scatter(
            g_qkv_w.astype(jnp.bfloat16), "fsdp", scatter_dimension=0, tiled=True
        ).astype(jnp.float32),
        lax.psum_scatter(
            g_qkv_b.astype(jnp.bfloat16), "fsdp", scatter_dimension=2, tiled=True
        ).astype(jnp.float32),
        lax.psum_scatter(
            g_out.astype(jnp.bfloat16), "fsdp", scatter_dimension=1, tiled=True
        ).astype(jnp.float32),
        lax.psum_scatter(
            g_gain_two.astype(jnp.bfloat16), "fsdp", scatter_dimension=0, tiled=True
        ).astype(jnp.float32),
        lax.psum_scatter(
            g_bias_two.astype(jnp.bfloat16), "fsdp", scatter_dimension=0, tiled=True
        ).astype(jnp.float32),
        lax.psum_scatter(
            g_gate_up.astype(jnp.bfloat16), "fsdp", scatter_dimension=0, tiled=True
        ).astype(jnp.float32),
        lax.psum_scatter(
            g_down.astype(jnp.bfloat16), "fsdp", scatter_dimension=1, tiled=True
        ).astype(jnp.float32),
    )
    return (d_middle + d_in_norm, shares)


def on_device(
    states,
    segment_ids,
    ln1_gain,
    ln1_bias,
    qkv_weight,
    qkv_bias,
    out_weight,
    ln2_gain,
    ln2_bias,
    gate_up_weight,
    down_weight,
    cotangent,
):
    rows = states.shape[0]
    places = jnp.arange(rows, dtype=jnp.int32)
    previous = jnp.concatenate([segment_ids[:1] - 1, segment_ids[:-1]])
    starts = lax.cummax(jnp.where(segment_ids != previous, places, jnp.zeros_like(places)), axis=0)
    position = places - starts
    half = ROT_DIM // 2
    inverse = rotary_base ** (-(jnp.arange(half, dtype=jnp.float32) * 2.0 / ROT_DIM))
    angle = position.astype(jnp.float32)[:, None] * inverse[None, :]
    cosine = jnp.cos(angle)[:, None, :]
    sine = jnp.sin(angle)[:, None, :]
    allowed = (segment_ids[:, None] == segment_ids[None, :]) & (places[None, :] <= places[:, None])
    residual_state = states.astype(jnp.float32)
    grad = cotangent.astype(jnp.float32)
    saved_list = []
    kept_list = []
    for layer in range(LAYERS):
        weights = fetch_forward(
            ln1_gain[layer],
            ln1_bias[layer],
            qkv_weight[layer],
            qkv_bias[layer],
            out_weight[layer],
            ln2_gain[layer],
            ln2_bias[layer],
            gate_up_weight[layer],
            down_weight[layer],
        )
        residual_state, saved = forward_layer(residual_state, weights, cosine, sine, allowed)
        saved_list.append(saved)
        kept_list.append(weights)
    out_states = residual_state.astype(jnp.bfloat16)
    share_list = [None] * LAYERS
    for layer in reversed(range(LAYERS)):
        weights = fetch_backward(
            ln1_gain[layer],
            ln1_bias[layer],
            qkv_weight[layer],
            qkv_bias[layer],
            out_weight[layer],
            ln2_gain[layer],
            ln2_bias[layer],
            gate_up_weight[layer],
            down_weight[layer],
        )
        grad, shares = backward_layer(grad, weights, saved_list[layer], cosine, sine, allowed)
        share_list[layer] = shares
    stacked = [
        jnp.stack([share_list[layer][index] for layer in range(LAYERS)]) for index in range(9)
    ]
    return (
        out_states,
        grad,
        stacked[0],
        stacked[1],
        stacked[2],
        stacked[3],
        stacked[4],
        stacked[5],
        stacked[6],
        stacked[7],
        stacked[8],
    )


def solution(mesh):
    in_specs = (
        P("fsdp", None),
        P("fsdp"),
        P(None, "fsdp"),
        P(None, "fsdp"),
        P(None, "fsdp", None, "tensor"),
        P(None, None, "tensor", "fsdp"),
        P(None, "tensor", "fsdp"),
        P(None, "fsdp"),
        P(None, "fsdp"),
        P(None, "fsdp", None, "tensor"),
        P(None, "tensor", "fsdp"),
        P("fsdp", None),
    )
    out_specs = (
        P("fsdp", None),
        P("fsdp", None),
        P(None, "fsdp"),
        P(None, "fsdp"),
        P(None, "fsdp", None, "tensor"),
        P(None, None, "tensor", "fsdp"),
        P(None, "tensor", "fsdp"),
        P(None, "fsdp"),
        P(None, "fsdp"),
        P(None, "fsdp", None, "tensor"),
        P(None, "tensor", "fsdp"),
    )
    return jax.shard_map(
        on_device, mesh=mesh, in_specs=in_specs, out_specs=out_specs, check_vma=False
    )
```

profile of v0, /device:TPU:17, one launch (start us, length us, event | category | flops | bytes accessed | tf_op | source)
XLA Modules:
  0.0 1804.7 jit_solution(12575819004488337822)
XLA Ops:
  17.8 9.4 all-gather
  28.4 8.8 all-gather.1
  38.5 9.3 all-gather.3
  51.6 9.2 all-gather.27.cloned.1.call-done
  60.8 8.5 fusion.92
  105.3 8.9 all-gather.5
  114.8 8.2 all-gather.6
  123.0 67.4 %all-reduce.21.cloned.1.call-done = bf16[576,2048]{1,0:T(8,128)(2,1)} async-done(((bf16[576,2048]{1,0:T(8,128)(2,1)}), bf16[576,2048]{1,0:T(8,128)(2,1)}) %all-reduce.21.cloned.1.call-update) | async-done | bytes 2359312 | tf_op jit(solution)/shard_map/psum | solution.py:154
  194.1 66.9 %all-gather.31.cloned.1.call-done = bf16[1,2048,2,1408]{3,1,2,0:T(8,128)(2,1)} async-done(((bf16[1,256,2,1408]{3,1,2,0:T(8,128)(2,1)}), bf16[1,2048,2,1408]{3,1,2,0:T(8,128)(2,1)}) %all-gather.31.cloned.1.call-update) | async-done | bytes 11534352 | tf_op jit(solution)/shard_map/all_gather | solution.py:77
  261.0 15.7 copy.117
  276.7 11.2 fusion.2
  292.8 14.9 all-gather.33.cloned.1.call-done
  307.7 8.4 fusion.76
  320.8 8.9 all-gather.9
  338.3 9.2 all-gather.12
  348.3 62.2 %all-reduce.23.cloned.1.call-done = bf16[576,2048]{1,0:T(8,128)(2,1)} async-done(((bf16[576,2048]{1,0:T(8,128)(2,1)}), bf16[576,2048]{1,0:T(8,128)(2,1)}) %all-reduce.23.cloned.1.call-update) | async-done | bytes 2359312 | tf_op jit(solution)/shard_map/psum | solution.py:169
  416.7 43.4 %all-gather.35.cloned.1.call-done = bf16[1,2048,3,512]{1,3,2,0:T(8,128)(2,1)} async-done(((bf16[1,256,3,512]{1,3,2,0:T(8,128)(2,1)}), bf16[1,2048,3,512]{1,3,2,0:T(8,128)(2,1)}) %all-gather.35.cloned.1.call-update) | async-done | bytes 6291472 | tf_op jit(solution)/shard_map/all_gather | solution.py:72
  460.0 8.4 fusion.95
  495.4 8.9 all-gather.14
  512.9 47.4 %all-gather.39.cloned.1.call-done = bf16[1,2048,2,1408]{3,1,2,0:T(8,128)(2,1)} async-done(((bf16[1,256,2,1408]{3,1,2,0:T(8,128)(2,1)}), bf16[1,2048,2,1408]{3,1,2,0:T(8,128)(2,1)}) %all-gather.39.cloned.1.call-update) | async-done | bytes 11534352 | tf_op jit(solution)/shard_map/all_gather | solution.py:77
  560.4 15.5 copy.124
  575.9 81.6 %all-reduce.25.cloned.1.call-done = bf16[576,2048]{1,0:T(8,128)(2,1)} async-done(((bf16[576,2048]{1,0:T(8,128)(2,1)}), bf16[576,2048]{1,0:T(8,128)(2,1)}) %all-reduce.25.cloned.1.call-update) | async-done | bytes 2359312 | tf_op jit(solution)/shard_map/psum | solution.py:154
  665.5 10.5 fusion
  676.0 28.7 %all-gather.41.cloned.1.call-done = bf16[1,1408,2048]{2,1,0:T(8,128)(2,1)} async-done(((bf16[1,1408,256]{2,1,0:T(8,128)(2,1)}), bf16[1,1408,2048]{2,1,0:T(8,128)(2,1)}) %all-gather.41.cloned.1.call-update) | async-done | bytes 5767184 | tf_op jit(solution)/shard_map/all_gather | solution.py:78
  704.7 9.7 fusion.100
  716.1 10.8 bitcast_convert_fusion.1
  727.0 94.3 %all-reduce.27.cloned.1.call-done = bf16[576,2048]{1,0:T(8,128)(2,1)} async-done(((bf16[576,2048]{1,0:T(8,128)(2,1)}), bf16[576,2048]{1,0:T(8,128)(2,1)}) %all-reduce.27.cloned.1.call-update) | async-done | bytes 2359312 | tf_op jit(solution)/shard_map/psum | solution.py:237
  835.5 11.4 multiply_reduce_fusion.1
  865.7 94.6 %all-reduce.29.cloned.1.call-done = bf16[576,2048]{1,0:T(8,128)(2,1)} async-done(((bf16[576,2048]{1,0:T(8,128)(2,1)}), bf16[576,2048]{1,0:T(8,128)(2,1)}) %all-reduce.29.cloned.1.call-update) | async-done | bytes 2359312 | tf_op jit(solution)/shard_map/psum | solution.py:282
  971.0 11.5 fusion.101
  982.6 9.7 bitcast_convert_fusion
  1006.1 81.0 %all-reduce.31.cloned.1.call-done = bf16[576,2048]{1,0:T(8,128)(2,1)} async-done(((bf16[576,2048]{1,0:T(8,128)(2,1)}), bf16[576,2048]{1,0:T(8,128)(2,1)}) %all-reduce.31.cloned.1.call-update) | async-done | bytes 2359312 | tf_op jit(solution)/shard_map/psum | solution.py:237
  1107.9 11.2 multiply_reduce_fusion
  1119.6 9.2 multiply_convert_fusion
  1142.6 9.6 convolution_convert_fusion.2
  1152.4 10.0 convolution_convert_fusion.3
  1163.2 11.2 convolution_convert_fusion.4
  1175.1 9.2 convolution_convert_fusion.5
  1185.0 15.8 convolution_convert_fusion
  1201.5 14.6 convolution_convert_fusion.1
  1227.1 124.5 %all-reduce.33.cloned.1.call-done = (bf16[576,2048]{1,0:T(8,128)(2,1)}, bf16[576,2048]{1,0:T(8,128)(2,1)}) async-done(((bf16[576,2048]{1,0:T(8,128)(2,1)}, bf16[576,2048]{1,0:T(8,128)(2,1)}), (bf16[576,2048]{1,0:T(8,128)(2,1)}, bf16[576,2048]{1,0:T(8,128)(2,1)})) %all-reduce.33.cloned.1.call-update) | async-done | bytes 4718608 | tf_op jit(solution)/shard_map/psum | solution.py:169
  1357.4 22.3 %all-reduce.11 = (bf16[2048]{0:T(1024)(128)(2,1)S(1)}, bf16[2048]{0:T(1024)(128)(2,1)S(1)}, bf16[2048]{0:T(1024)(128)(2,1)S(1)}, bf16[2048]{0:T(1024)(128)(2,1)S...) all-reduce(bf16[2048]{0:T(1024)(128)(2,1)S(1)} %copy-done.75, ...), channel_id=21, replica_groups=mesh['fsdp'=8,'tensor'=4] {'fsdp'}, use_global_device_ids=true, to_apply=%region_35.36.clone | all-reduce | flops 19456 | bytes 77824
  1394.1 20.4 %reduce-scatter.25.cloned.1.call-done = bf16[1408,256]{1,0:T(8,128)(2,1)} async-done(((bf16[1408,2048]{1,0:T(8,128)(2,1)}), bf16[1408,256]{1,0:T(8,128)(2,1)}) %reduce-scatter.25.cloned.1.call-update) | async-done | bytes 720912 | tf_op jit(solution)/shard_map/reduce_scatter | solution.py:316
  1414.5 62.9 %reduce-scatter.23.cloned.1.call-done = bf16[1408,256]{1,0:T(8,128)(2,1)} async-done(((bf16[1408,2048]{1,0:T(8,128)(2,1)}), bf16[1408,256]{1,0:T(8,128)(2,1)}) %reduce-scatter.23.cloned.1.call-update) | async-done | bytes 720912 | tf_op jit(solution)/shard_map/reduce_scatter | solution.py:316
  1480.5 61.9 %reduce-scatter.13.cloned.1.call-done = bf16[256,3,512]{2,0,1:T(8,128)(2,1)} async-done(((bf16[2048,3,512]{2,0,1:T(8,128)(2,1)}), bf16[256,3,512]{2,0,1:T(8,128)(2,1)}) %reduce-scatter.13.cloned.1.call-update) | async-done | bytes 786448 | tf_op jit(solution)/shard_map/reduce_scatter | solution.py:298
  1542.4 65.5 %reduce-scatter.11.cloned.1.call-done = bf16[256,3,512]{2,0,1:T(8,128)(2,1)} async-done(((bf16[2048,3,512]{2,0,1:T(8,128)(2,1)}), bf16[256,3,512]{2,0,1:T(8,128)(2,1)}) %reduce-scatter.11.cloned.1.call-update) | async-done | bytes 786448 | tf_op jit(solution)/shard_map/reduce_scatter | solution.py:298
  1611.2 87.1 %reduce-scatter.21.cloned.1.call-done = bf16[256,2,1408]{2,0,1:T(8,128)(2,1)} async-done(((bf16[2048,2,1408]{2,0,1:T(8,128)(2,1)}), bf16[256,2,1408]{2,0,1:T(8,128)(2,1)}) %reduce-scatter.21.cloned.1.call-update) | async-done | bytes 1441808 | tf_op jit(solution)/shard_map/reduce_scatter | solution.py:313
  1698.2 90.3 %reduce-scatter.19.cloned.1.call-done = bf16[256,2,1408]{2,0,1:T(8,128)(2,1)} async-done(((bf16[2048,2,1408]{2,0,1:T(8,128)(2,1)}), bf16[256,2,1408]{2,0,1:T(8,128)(2,1)}) %reduce-scatter.19.cloned.1.call-update) | async-done | bytes 1441808 | tf_op jit(solution)/shard_map/reduce_scatter | solution.py:313
  (432 shorter events, 266.8 us)
Async XLA Ops:
  7.2 53.6 %all-gather.27.cloned.1.call-start = ((), (), s32[]{:S(2)}) async-start(), calls=%async_computation.22 | async-start | bytes 7077888 | tf_op jit(solution)/shard_map/all_gather | solution.py:72
  9.8 18.0 copy-start.83
  9.8 28.0 %copy-start.76 = (bf16[2,3,8,8]{3,2,1,0:T(8,128)(2,1)S(1)}, bf16[2,3,8,8]{3,2,1,0:T(8,128)(2,1)}, u32[]{:S(2)}) copy-start(bf16[2,3,8,8]{3,2,1,0:T(8,128)(2,1)} %param.17) | copy-start | bytes 2308
  12.2 79.3 %all-gather.29.cloned.1.call-start = ((), (), s32[]{:S(2)}) async-start(), calls=%async_computation.23 | async-start | bytes 2359296 | tf_op jit(solution)/shard_map/all_gather | solution.py:74
  14.1 176.4 %all-reduce.21.cloned.1.call-start = ((), (), s32[]{:S(2)}) async-start(), calls=%async_computation.8 | async-start | bytes 4718592 | tf_op jit(solution)/shard_map/psum | solution.py:154
  15.5 61.5 %copy-start.30 = (pred[576,576]{0,1:T(8,128)(4,1)}, pred[576,576]{0,1:T(8,128)(4,1)S(1)}, u32[]{:S(2)}) copy-start(pred[576,576]{0,1:T(8,128)(4,1)S(1)} %fusion.102) | copy-start | bytes 995332
  15.9 34.8 %copy-start.62 = (f32[576]{0:T(1024)}, f32[576]{0:T(1024)S(1)}, u32[]{:S(2)}) copy-start(f32[576]{0:T(1024)S(1)} %broadcast_multiply_fusion.11) | copy-start | bytes 6916
  51.5 25.3 %copy-start.26 = (f32[576,8]{0,1:T(8,128)}, f32[576,8]{0,1:T(8,128)S(1)}, u32[]{:S(2)}) copy-start(f32[576,8]{0,1:T(8,128)S(1)} %get-tuple-element.141) | copy-start | bytes 55300
  51.6 25.3 %copy-start.28 = (f32[576,8]{0,1:T(8,128)}, f32[576,8]{0,1:T(8,128)S(1)}, u32[]{:S(2)}) copy-start(f32[576,8]{0,1:T(8,128)S(1)} %get-tuple-element.142) | copy-start | bytes 55300
  96.1 164.9 %all-gather.31.cloned.1.call-start = ((), (), s32[]{:S(2)}) async-start(), calls=%async_computation.24 | async-start | bytes 12976128 | tf_op jit(solution)/shard_map/all_gather | solution.py:77
  102.1 205.6 %all-gather.33.cloned.1.call-start = ((), (), s32[]{:S(2)}) async-start(), calls=%async_computation.25 | async-start | bytes 6488064 | tf_op jit(solution)/shard_map/all_gather | solution.py:78
  104.7 305.8 %all-reduce.23.cloned.1.call-start = ((), (), s32[]{:S(2)}) async-start(), calls=%async_computation.9 | async-start | bytes 4718592 | tf_op jit(solution)/shard_map/psum | solution.py:169
  114.2 162.5 %copy-start.51 = (f32[1,2048]{1,0:T(1,128)}, f32[1,2048]{1,0:T(1,128)S(1)}, u32[]{:S(2)}) copy-start(f32[1,2048]{1,0:T(1,128)S(1)} %convert_element_type.369) | copy-start | bytes 24580
  123.0 153.7 %copy-start.78 = (f32[1,2048]{1,0:T(1,128)}, f32[1,2048]{1,0:T(1,128)S(1)}, u32[]{:S(2)}) copy-start(f32[1,2048]{1,0:T(1,128)S(1)} %convert_element_type.370) | copy-start | bytes 24580
  193.0 83.7 %copy-start.56 = (f32[576]{0:T(1024)}, f32[576]{0:T(1024)S(1)}, u32[]{:S(2)}) copy-start(f32[576]{0:T(1024)S(1)} %broadcast_multiply_fusion.10) | copy-start | bytes 6916
  194.1 82.6 %copy-start.64 = (f32[576]{0:T(1024)}, f32[576]{0:T(1024)S(1)}, u32[]{:S(2)}) copy-start(f32[576]{0:T(1024)S(1)} %add_rsqrt_fusion.2) | copy-start | bytes 6916
  316.0 22.2 %copy-start.73 = (bf16[1,3,8,8]{3,2,1,0:T(8,128)(2,1)S(1)}, bf16[1,3,8,8]{3,2,1,0:T(8,128)(2,1)}, u32[]{:S(2)}) copy-start(bf16[1,3,8,8]{3,2,1,0:T(8,128)(2,1)} %get-tuple-element.139) | copy-start | bytes 1156
  316.0 144.0 %all-gather.35.cloned.1.call-start = ((), (), s32[]{:S(2)}) async-start(), calls=%async_computation.26 | async-start | bytes 7077888 | tf_op jit(solution)/shard_map/all_gather | solution.py:72
  317.3 172.9 %all-gather.37.cloned.1.call-start = ((), (), s32[]{:S(2)}) async-start(), calls=%async_computation.27 | async-start | bytes 2359296 | tf_op jit(solution)/shard_map/all_gather | solution.py:74
  318.0 242.3 %all-gather.39.cloned.1.call-start = ((), (), s32[]{:S(2)}) async-start(), calls=%async_computation.28 | async-start | bytes 12976128 | tf_op jit(solution)/shard_map/all_gather | solution.py:77
  320.7 336.7 %all-reduce.25.cloned.1.call-start = ((), (), s32[]{:S(2)}) async-start(), calls=%async_computation.10 | async-start | bytes 4718592 | tf_op jit(solution)/shard_map/psum | solution.py:154
  416.6 51.8 %copy-start.66 = (f32[576]{0:T(1024)}, f32[576]{0:T(1024)S(1)}, u32[]{:S(2)}) copy-start(f32[576]{0:T(1024)S(1)} %add_rsqrt_fusion.1) | copy-start | bytes 6916
  494.6 210.1 %all-gather.41.cloned.1.call-start = ((), (), s32[]{:S(2)}) async-start(), calls=%async_computation.29 | async-start | bytes 6488064 | tf_op jit(solution)/shard_map/all_gather | solution.py:78
  495.4 326.0 %all-reduce.27.cloned.1.call-start = ((), (), s32[]{:S(2)}) async-start(), calls=%async_computation.11 | async-start | bytes 4718592 | tf_op jit(solution)/shard_map/psum | solution.py:237
  504.3 157.5 %copy-start.53 = (f32[1,2048]{1,0:T(1,128)}, f32[1,2048]{1,0:T(1,128)S(1)}, u32[]{:S(2)}) copy-start(f32[1,2048]{1,0:T(1,128)S(1)} %convert_element_type.373) | copy-start | bytes 24580
  665.5 39.2 %copy-start.17 = (bf16[576,2048]{1,0:T(8,128)(2,1)S(1)}, bf16[576,2048]{1,0:T(8,128)(2,1)}, u32[]{:S(2)}) copy-start(bf16[576,2048]{1,0:T(8,128)(2,1)} %param.23) | copy-start | bytes 7077892
  716.0 105.3 %copy-start.54 = (f32[1,2048]{1,0:T(1,128)S(1)}, f32[1,2048]{1,0:T(1,128)}, u32[]{:S(2)}) copy-start(f32[1,2048]{1,0:T(1,128)} %copy-done.53) | copy-start | bytes 24580
  716.0 105.3 %copy-start.60 = (f32[576]{0:T(1024)S(1)}, f32[576]{0:T(1024)}, u32[]{:S(2)}) copy-start(f32[576]{0:T(1024)} %copy-done.59) | copy-start | bytes 6916
  716.0 105.3 %copy-start.69 = (f32[576]{0:T(1024)S(1)}, f32[576]{0:T(1024)}, u32[]{:S(2)}) copy-start(f32[576]{0:T(1024)} %copy-done.68) | copy-start | bytes 6916
  726.9 233.4 %all-reduce.29.cloned.1.call-start = ((), (), s32[]{:S(2)}) async-start(), calls=%async_computation.12 | async-start | bytes 4718592 | tf_op jit(solution)/shard_map/psum | solution.py:282
  860.4 99.9 %copy-start.67 = (f32[576]{0:T(1024)S(1)}, f32[576]{0:T(1024)}, u32[]{:S(2)}) copy-start(f32[576]{0:T(1024)} %copy-done.66) | copy-start | bytes 6916
  865.5 221.5 %all-reduce.31.cloned.1.call-start = ((), (), s32[]{:S(2)}) async-start(), calls=%async_computation.13 | async-start | bytes 4718592 | tf_op jit(solution)/shard_map/psum | solution.py:237
  992.3 232.7 %reduce-scatter.17.cloned.1.call-start = ((), (), s32[]{:S(2)}) async-start(), calls=%async_computation.17 | async-start | bytes 2359296 | tf_op jit(solution)/shard_map/reduce_scatter | solution.py:304
  1000.2 86.9 %copy-start.1 = (bf16[576,2048]{1,0:T(8,128)(2,1)S(1)}, bf16[576,2048]{1,0:T(8,128)(2,1)}, u32[]{:S(2)}) copy-start(bf16[576,2048]{1,0:T(8,128)(2,1)} %param.12) | copy-start | bytes 7077892
  1000.2 86.9 %copy-start.52 = (f32[1,2048]{1,0:T(1,128)S(1)}, f32[1,2048]{1,0:T(1,128)}, u32[]{:S(2)}) copy-start(f32[1,2048]{1,0:T(1,128)} %copy-done.51) | copy-start | bytes 24580
  1000.2 86.9 %copy-start.57 = (f32[576]{0:T(1024)S(1)}, f32[576]{0:T(1024)}, u32[]{:S(2)}) copy-start(f32[576]{0:T(1024)} %copy-done.56) | copy-start | bytes 6916
  1000.2 86.9 %copy-start.65 = (f32[576]{0:T(1024)S(1)}, f32[576]{0:T(1024)}, u32[]{:S(2)}) copy-start(f32[576]{0:T(1024)} %copy-done.64) | copy-start | bytes 6916
  1005.8 219.2 %reduce-scatter.15.cloned.1.call-start = ((), (), s32[]{:S(2)}) async-start(), calls=%async_computation.16 | async-start | bytes 2359296 | tf_op jit(solution)/shard_map/reduce_scatter | solution.py:304
  1119.1 232.5 %all-reduce.33.cloned.1.call-start = ((), (), s32[]{:S(2)}) async-start(), calls=%async_computation.30 | async-start | bytes 9437184 | tf_op jit(solution)/shard_map/psum | solution.py:169
  1142.5 272.0 %reduce-scatter.25.cloned.1.call-start = ((), (), s32[]{:S(2)}) async-start(), calls=%async_computation.21 | async-start | bytes 6488064 | tf_op jit(solution)/shard_map/reduce_scatter | solution.py:316
  1152.2 325.2 %reduce-scatter.23.cloned.1.call-start = ((), (), s32[]{:S(2)}) async-start(), calls=%async_computation.20 | async-start | bytes 6488064 | tf_op jit(solution)/shard_map/reduce_scatter | solution.py:316
  1162.5 379.9 %reduce-scatter.13.cloned.1.call-start = ((), (), s32[]{:S(2)}) async-start(), calls=%async_computation.15 | async-start | bytes 7077888 | tf_op jit(solution)/shard_map/reduce_scatter | solution.py:298
  1174.4 433.5 %reduce-scatter.11.cloned.1.call-start = ((), (), s32[]{:S(2)}) async-start(), calls=%async_computation.14 | async-start | bytes 7077888 | tf_op jit(solution)/shard_map/reduce_scatter | solution.py:298
  1184.3 513.9 %reduce-scatter.21.cloned.1.call-start = ((), (), s32[]{:S(2)}) async-start(), calls=%async_computation.19 | async-start | bytes 12976128 | tf_op jit(solution)/shard_map/reduce_scatter | solution.py:313
  1200.8 587.7 %reduce-scatter.19.cloned.1.call-start = ((), (), s32[]{:S(2)}) async-start(), calls=%async_computation.18 | async-start | bytes 12976128 | tf_op jit(solution)/shard_map/reduce_scatter | solution.py:313
  1224.9 132.4 %copy-start.72 = (bf16[3,8,64]{2,1,0:T(8,128)(2,1)S(1)}, bf16[3,8,64]{2,1,0:T(8,128)(2,1)}, u32[]{:S(2)}) copy-start(bf16[3,8,64]{2,1,0:T(8,128)(2,1)} %get-tuple-element.92) | copy-start | bytes 9220
  1224.9 132.4 %copy-start.74 = (bf16[2048]{0:T(1024)(128)(2,1)S(1)}, bf16[2048]{0:T(1024)(128)(2,1)}, u32[]{:S(2)}) copy-start(bf16[2048]{0:T(1024)(128)(2,1)} %get-tuple-element.68) | copy-start | bytes 12292
  1225.0 132.4 %copy-start.75 = (bf16[2048]{0:T(1024)(128)(2,1)S(1)}, bf16[2048]{0:T(1024)(128)(2,1)}, u32[]{:S(2)}) copy-start(bf16[2048]{0:T(1024)(128)(2,1)} %get-tuple-element.70) | copy-start | bytes 12292
  (86 other events, 450.0 us)
Sparse Core Ops, SparseCore 0:
  12.3 48.4 all-gather.26
  63.2 28.1 all-gather.28
  96.2 94.2 all-reduce.20
  192.8 68.0 all-gather.30
  263.3 44.3 all-gather.32
  316.2 94.2 all-reduce.22
  412.9 47.0 all-gather.34
  461.9 28.1 all-gather.36
  492.6 67.7 all-gather.38
  563.2 94.2 all-reduce.24
  659.9 44.7 all-gather.40
  727.0 94.2 all-reduce.26
  865.6 94.6 all-reduce.28
  992.4 94.6 all-reduce.30
  1090.8 41.2 reduce-scatter.16
  1135.5 41.2 reduce-scatter.14
  1180.2 171.3 all-reduce.32
  1355.4 59.0 reduce-scatter.24
  1418.3 59.0 reduce-scatter.22
  1480.6 61.7 reduce-scatter.12
  1546.2 61.7 reduce-scatter.10
  1611.4 86.7 reduce-scatter.20
  1701.7 86.7 reduce-scatter.18
where the time goes:
time: 1810 us; the launch traced here: 1800 us
  waiting for transfers between devices  1210 us (67%)
  matrix products  246 us (14%)
  blocking collectives  110 us (6%)
  local copies, waits for them, and re-layouts  108 us (6%)
  other arithmetic  107 us (6%)
    psum x2, waiting for transfers between devices, forward_layer(): lax.psum(ff_part.astype(jnp.bfloat16), 'tensor').astype(jnp.float32)  187 us
    reduce_scatter x2, waiting for transfers between devices, backward_layer(): lax.psum_scatter(g_gate_up.astype(jnp.bfloat16), 'fsdp', scatter_dimensio...  177 us
    psum x2, waiting for transfers between devices, backward_layer(): lax.psum(ff_back.astype(jnp.bfloat16), 'tensor').astype(jnp.float32)  175 us
    psum x2, waiting for transfers between devices, forward_layer(): lax.psum(attn_part.astype(jnp.bfloat16), 'tensor').astype(jnp.float32)  149 us
    reduce_scatter x2, waiting for transfers between devices, backward_layer(): lax.psum_scatter(g_qkv_w.astype(jnp.bfloat16), 'fsdp', scatter_dimension=...  127 us
    all_gather x2, waiting for transfers between devices, fetch_forward(): lax.all_gather(gate_up_w, 'fsdp', axis=0, tiled=True)  114 us
    psum x1, waiting for transfers between devices, backward_layer(): lax.psum(attn_back.astype(jnp.bfloat16), 'tensor').astype(jnp.float32)  94.6 us
    reduce_scatter x2, waiting for transfers between devices, backward_layer(): lax.psum_scatter(g_down.astype(jnp.bfloat16), 'fsdp', scatter_dimension=1...  83.3 us
  transfers between devices with their start and end apart: 23, of which 21 were waited for; matrix products, arithmetic and copies ran while one was open for 17% of the time, Pallas kernels for 0%

commit v1 on v0

v1 whole, which is shorter than its diff:
```python
import functools
import math

import jax
import jax.numpy as jnp
from jax import lax
from jax.experimental import pallas as pl
from jax.experimental.pallas import tpu as pltpu
from jax.sharding import PartitionSpec as P

MESH = pl.DeviceIdType.MESH
HEAD_DIM = 64
ROT_DIM = 16
LAYERS = 2
PAIR = 2 * HEAD_DIM
ANY = pl.BlockSpec(memory_space=pl.ANY)
VMEM = pl.BlockSpec(memory_space=pltpu.VMEM)
BF16 = jnp.bfloat16
F32 = jnp.float32

norm_epsilon = 1e-05
rotary_base = 10000.0


def dot(a, b):
    return lax.dot_general(a, b, (((1,), (0,)), ((), ())), preferred_element_type=F32)


def dot_nt(a, b):
    return lax.dot_general(a, b, (((1,), (1,)), ((), ())), preferred_element_type=F32)


def dot_tn(a, b):
    return lax.dot_general(a, b, (((0,), (0,)), ((), ())), preferred_element_type=F32)


def tiles(extent, most=512):
    return [(at, min(most, extent - at)) for at in range(0, extent, most)]


def standardize(values):
    average = jnp.mean(values, axis=-1, keepdims=True)
    centred = values - average
    spread = jnp.mean(centred * centred, axis=-1, keepdims=True)
    rstd = lax.rsqrt(spread + norm_epsilon)
    return centred * rstd, rstd


def turn(values, rope, sign):
    half = ROT_DIM // 2
    factor, below, above = rope
    return values * factor + sign * (
        pltpu.roll(values, PAIR - half, 1) * below + pltpu.roll(values, half, 1) * above
    )


def when(condition):
    return pl.when(condition)


def to(source, target, send, arrive, place):
    return pltpu.make_async_remote_copy(
        src_ref=source, dst_ref=target, send_sem=send, recv_sem=arrive, device_id=place, device_id_type=MESH
    )


def spread(build, source, target, count=4):
    rows = source.shape[-2] // count
    for r in range(count):
        piece = (slice(None),) * (len(source.shape) - 2) + (pl.ds(r * rows, rows), slice(None))
        build(source.at[piece], target.at[piece]).start()


def start(source, target, build):
    spread(build, source, target)


def whole(source, target, build):
    return build(source, target)


class Line:
    def __init__(self, count):
        place = lax.axis_index("tensor")
        half = count // 2
        left = place < half
        self.inner = jnp.where(left, place + 1, place - 1)
        self.outer = jnp.where(left, place - 1, place + 1)
        self.has_outer = (place != 0) & (place != count - 1)
        self.no_outer = jnp.logical_not(self.has_outer)
        self.distance = jnp.where(left, half - 1 - place, place - half)
        self.centre = self.distance == 0
        self.off_centre = jnp.logical_not(self.centre)


class Group:
    def __init__(self, count):
        self.count = count
        self.chips = count // 2
        self.me = lax.axis_index("fsdp")
        self.chip = self.me // 2
        self.core = self.me % 2
        self.peer = self.me + 1 - 2 * self.core
        self.square = self.chips == 4
        self.everyone = [(self.me + i) % count for i in range(1, count)]
        if self.square:
            self.x = self.at(self.chip + 1 - 2 * (self.chip % 2))
            self.y = self.at(self.chip + 2 - 4 * (self.chip // 2))
            self.far = self.at(3 - self.chip)
            self.others = [self.x, self.y]
        else:
            self.others = [self.at((self.chip + i) % self.chips) for i in range(1, self.chips)]

    def at(self, chip):
        return chip * 2 + self.core


def enter(line, partners):
    barrier = pltpu.get_barrier_semaphore()
    for partner in partners:
        pl.semaphore_signal(barrier, inc=1, device_id={"fsdp": partner}, device_id_type=MESH)
    pl.semaphore_signal(barrier, inc=1, device_id={"tensor": line.inner}, device_id_type=MESH)

    @when(line.has_outer)
    def _():
        pl.semaphore_signal(barrier, inc=1, device_id={"tensor": line.outer}, device_id_type=MESH)
        pl.semaphore_wait(barrier, len(partners) + 2)

    @when(line.no_outer)
    def _():
        pl.semaphore_wait(barrier, len(partners) + 1)


class Flow:
    def __init__(self, line, steps, span, rows, refs):
        self.line, self.steps, self.span, self.rows = line, steps, span, rows
        self.from_outer, self.from_inner, self.running = refs[:3]
        self.send_in, self.got_out, self.send_out, self.got_in, self.credit = refs[3:]
        self.lag = jnp.minimum(3 * line.distance + 2, steps - 1)

    def slot(self, i):
        big = self.rows * self.span
        return pl.ds(pl.multiple_of(i * big, big), big)

    def pieces(self, i):
        for r in range(self.span):
            q = i * self.span + r
            yield q, pl.ds(pl.multiple_of(q * self.rows, self.rows), self.rows)

    def inward(self, q, here, target, arrive):
        return to(
            self.running.at[here], target.at[here], self.send_in.at[q], arrive.at[q], {"tensor": self.line.inner}
        )

    def outward(self, q, here):
        return to(
            self.from_inner.at[here], self.from_inner.at[here], self.send_out.at[q], self.got_in.at[q],
            {"tensor": self.line.outer},
        )

    def clear(self, i):
        for q, here in self.pieces(i):
            self.inward(q, here, self.from_inner, self.got_in).wait_send()

    def push(self, i, again):
        line = self.line

        @when(line.centre & again)
        def _():
            pl.semaphore_wait(self.credit, 1)

        for q, here in self.pieces(i):

            @when(line.has_outer)
            def _(q=q, here=here):
                self.inward(q, here, self.from_outer, self.got_out).wait_recv()
                total = self.running[here, :].astype(F32) + self.from_outer[here, :].astype(F32)
                self.running[here, :] = total.astype(BF16)

            @when(line.centre)
            def _(q=q, here=here):
                self.inward(q, here, self.from_inner, self.got_in).start()

            @when(line.off_centre)
            def _(q=q, here=here):
                self.inward(q, here, self.from_outer, self.got_out).start()

    def pull(self, i):
        line = self.line
        for q, here in self.pieces(i):
            self.inward(q, here, self.from_inner, self.got_in).wait_recv()

            @when(line.centre)
            def _(q=q, here=here):
                total = self.running[here, :].astype(F32) + self.from_inner[here, :].astype(F32)
                self.from_inner[here, :] = total.astype(BF16)

            @when(line.has_outer)
            def _(q=q, here=here):
                self.outward(q, here).start()

    def release(self, i, more):
        line = self.line

        @when(line.has_outer)
        def _():
            for q, here in self.pieces(i):
                self.outward(q, here).wait_send()

        @when(line.centre & more)
        def _():
            pl.semaphore_signal(self.credit, inc=1, device_id={"tensor": line.inner}, device_id_type=MESH)


def flow_scratch(steps, span, tokens, width):
    whole = pltpu.VMEM((tokens, width), BF16)
    sems = pltpu.SemaphoreType.DMA((steps * span,))
    return [whole, whole, whole, sems, sems, sems, sems, pltpu.SemaphoreType.REGULAR]


def gather_kinds(count):
    return 9 if count == 8 else count


class Gather:
    def __init__(self, group, own, whole, send, arrive, load):
        self.group, self.own, self.whole, self.send, self.arrive, self.load_sems = group, own, whole, send, arrive, load
        self.half = own.shape[1] // 2
        self.links = len(group.others)

    def half_at(self, shard, h):
        return self.whole.at[shard, :, pl.ds(h * self.half, self.half), :]

    def way(self, kind):
        g, links = self.group, self.links
        if kind < links:
            return self.own, self.whole.at[g.me], g.others[kind]
        if kind == links:
            return self.own, self.whole.at[g.me], g.peer
        if kind <= 2 * links:
            shard = self.whole.at[g.others[kind - links - 1]]
            return shard, shard, g.peer
        if kind == 2 * links + 1:
            return self.half_at(g.x, 0), self.half_at(g.x, 0), g.y
        if kind == 2 * links + 2:
            return self.half_at(g.y, 1), self.half_at(g.y, 1), g.x
        return self.whole.at[g.far], self.whole.at[g.far], g.peer

    def build(self, kind, source, target):
        return to(source, target, self.send.at[kind], self.arrive.at[kind], {"fsdp": self.way(kind)[2]})

    def copy(self, kind):
        return self.build(kind, *self.way(kind)[:2])

    def start(self, kind):
        spread(functools.partial(self.build, kind), *self.way(kind)[:2])

    def local(self):
        return pltpu.make_async_copy(self.own, self.whole.at[self.group.me], self.send.at[gather_kinds(self.group.count) - 1])

    def begin(self):
        for kind in range(self.links + 1):
            self.start(kind)
        self.local().start()

    def relay(self):
        for kind in range(self.links):
            self.copy(kind).wait_recv()
        if self.group.square:
            self.start(2 * self.links + 1)
            self.start(2 * self.links + 2)
        for kind in range(self.links):
            self.start(self.links + 1 + kind)

    def relay_far(self):
        if self.group.square:
            self.copy(2 * self.links + 1).wait_recv()
            self.copy(2 * self.links + 2).wait_recv()
            self.start(2 * self.links + 3)

    def settle(self):
        self.local().wait()
        for kind in range(self.links, 2 * self.links + 1):
            self.copy(kind).wait_recv()
        if self.group.square:
            self.copy(2 * self.links + 3).wait_recv()

    def loads(self, target):
        depth = self.own.shape[1]
        for k in range(self.group.count):
            yield pltpu.make_async_copy(
                self.whole.at[k], target.at[:, pl.ds(k * depth, depth), :], self.load_sems.at[k]
            )

    def finish(self):
        for kind in range(2 * self.links + 1 + (3 if self.group.square else 0)):
            self.copy(kind).wait_send()


def train_kernel(
    count, shards, steps, span, per_step,
    states, cotangent, own_norms, own_bias, rope, mask, own_q, own_o, own_g, own_d,
    out_states, grad_states, sums_attn, sums_ffn, norm_parts, bias_parts,
    whole_q, whole_o, whole_g, whole_d, s_x, s_n, s_y, s_qkv, s_att, s_gu, s_hid,
    mate_attn, mate_ffn, via_attn, via_ffn,
    res, w_attn, w_ffn, gu, hid, qkv, att, d_key, d_value, x_in, low,
    norms, biases, bias_in, norm_acc, bias_acc, columns, turned, staged,
    x_save, x_sem, low_sem, out_sem, keep_sem, act_sem, misc, load_sem, g_send, g_arrive,
    column_sem, stage_sem, relay_sem, mate_send, mate_got, own_send, own_got, small_send, small_got,
    *flow_refs,
):
    tokens, width = res.shape
    big = tokens // steps
    local, ff = w_attn.shape[2], w_ffn.shape[2]
    depth = width // shards
    line = Line(count)
    group = Group(shards)
    chips = group.chips
    flow = Flow(line, steps, span, big // span, flow_refs)
    scale = 1.0 / math.sqrt(HEAD_DIM)
    half = 2 * LAYERS
    stages = 2 * half
    total = stages * steps
    top = LAYERS - 1
    units = 2 * chips

    def block(c):
        return pl.ds(pl.multiple_of(c * big, big), big)

    kinds = [(own_q, whole_q), (own_o, whole_o), (own_g, whole_g), (own_d, whole_d)]
    targets = [w_attn.at[0:3], w_attn.at[3:4], w_ffn.at[0:2], w_ffn.at[2:3]]

    def gather(layer, kind):
        n = 4 * layer + kind
        own, whole = kinds[kind]
        return Gather(group, own.at[layer], whole.at[layer], g_send.at[n], g_arrive.at[n], load_sem.at[kind])

    def load(layer, kind, wait):
        own, whole = kinds[kind]
        way = Gather(group, own.at[0], whole.at[layer], g_send.at[0], g_arrive.at[0], load_sem.at[kind])
        for copy in way.loads(targets[kind]):
            if wait:
                copy.wait()
            else:
                copy.start()

    events = {}

    def event(t, where, *actions):
        events.setdefault((t, where, None), []).extend(actions)

    def event_by_role(centre, others, *actions):
        events.setdefault(centre + (True,), []).extend(actions)
        events.setdefault(others + (False,), []).extend(actions)

    def loading(layer, kind, wait):
        return functools.partial(load, layer, kind, wait)

    def at(stage, i):
        return stage * steps + min(i, steps - 1)

    q, o, g, d = 0, 1, 2, 3
    event(0, 1, gather(0, o).relay_far, gather(0, o).settle, loading(0, o, False), loading(0, o, True))
    event_by_role((at(0, 3), 0), (at(0, 4), 0), gather(0, g).relay)
    event_by_role((at(0, 5), 0), (at(0, 5), 2), gather(0, g).relay_far, gather(0, d).begin)
    event(at(1, 0), 0, gather(0, g).settle, loading(0, g, False), loading(0, g, True))
    event(at(1, 0), 1, gather(0, d).relay)
    for layer in range(1, LAYERS):
        s = 2 * layer - 1
        event(at(s, 0), 1, gather(layer, q).begin)
        if layer == 1:
            event(at(s, 0), 1, gather(0, d).relay_far, gather(0, d).settle, loading(0, d, False), loading(0, d, True))
        event(at(s, 2), 0, gather(layer, q).relay, gather(layer, o).begin)
        event_by_role((at(s, 3), 0), (at(s, 3), 2), gather(layer, q).relay_far, gather(layer, o).relay, gather(layer, g).begin)
        event(at(s, 4), 2, gather(layer, o).relay_far)
        event(at(s, 5), 2, gather(layer, q).settle, loading(layer, q, False))
        event(at(s, 5), 2, gather(layer, o).settle, loading(layer, o, False))
        s += 1
        event(at(s, 0), 0, loading(layer, q, True), loading(layer, o, True))
        event_by_role((at(s, 0), 0), (at(s, 0), 2), gather(layer, g).relay)
        event_by_role((at(s, 2), 0), (at(s, 2), 2), gather(layer, g).relay_far, gather(layer, d).begin)
        event(at(s, 3), 2, gather(layer, g).settle, loading(layer, g, False))
        event_by_role((at(s, 4), 0), (at(s, 4), 2), gather(layer, d).relay)
        event(at(s, 5), 2, gather(layer, d).relay_far)
        s += 1
        event(at(s, 0), 0, loading(layer, g, True), gather(layer, d).settle, loading(layer, d, False))
        event(at(s, 0), 1, loading(layer, d, True))

    def run_events(t, where):
        ordered = sorted(events.items(), key=lambda item: item[0][:2])
        ordered = [(at, role, actions) for (at, place, role), actions in ordered if place == where]
        for stage in sorted({at // steps for at, _, _ in ordered}):

            @when(t // steps == stage)
            def _(stage=stage):
                for at, role, actions in ordered:
                    if at // steps != stage:
                        continue
                    condition = t == at
                    if role is not None:
                        condition = condition & (line.centre if role else line.off_centre)

                    @when(condition)
                    def _(actions=actions):
                        for action in actions:
                            action()

    enter(line, group.everyone)
    mine = pl.ds(pl.multiple_of(group.me * depth, depth), depth)
    small = []
    for n, other in enumerate(group.everyone):
        sems = (small_send.at[0, n], small_got.at[0, n])
        small.append(to(own_norms, norms.at[:, mine], *sems, {"fsdp": other}))
        sems = (small_send.at[1, n], small_got.at[1, n])
        small.append(to(own_bias, bias_in.at[group.me], *sems, {"fsdp": other}))
    gather(0, q).begin()
    for copy in small:
        copy.start()
    starts = [
        pltpu.make_async_copy(own_norms, norms.at[:, mine], misc.at[0]),
        pltpu.make_async_copy(own_bias, bias_in.at[group.me], misc.at[1]),
        pltpu.make_async_copy(states, flow.running, misc.at[2]),
        pltpu.make_async_copy(cotangent, s_y.at[0], misc.at[3]),
    ]
    for copy in starts:
        copy.start()
    qkv[...] = jnp.zeros_like(qkv)
    norm_acc[...] = jnp.zeros_like(norm_acc)
    bias_acc[...] = jnp.zeros_like(bias_acc)
    for copy in starts:
        copy.wait()
    for c in range(steps):
        res[c * big : (c + 1) * big, :] = flow.running[c * big : (c + 1) * big, :].astype(F32)
    for copy in small:
        copy.wait_recv()
    each = HEAD_DIM // shards
    source = lax.broadcasted_iota(jnp.int32, (PAIR, local), 0)
    column = lax.broadcasted_iota(jnp.int32, (PAIR, local), 1)
    at_head = lax.div(source, each) == lax.div(column, HEAD_DIM)
    whole_bias = jnp.zeros((8, local), F32)
    for k in range(shards):
        match = at_head & (lax.rem(column, HEAD_DIM) == k * each + lax.rem(source, each))
        whole_bias += dot(bias_in[k].astype(BF16), jnp.where(match, 1.0, 0.0).astype(BF16))
    biases[...] = whole_bias
    gather(0, q).relay()
    gather(0, o).begin()
    gather(0, q).relay_far()
    gather(0, o).relay()
    gather(0, g).begin()
    gather(0, q).settle()
    load(0, q, False)
    load(0, q, True)

    lanes = lax.broadcasted_iota(jnp.int32, (big, PAIR), 1)
    first_head = lanes < HEAD_DIM

    def save_x(stage, c):
        return pltpu.make_async_copy(res.at[block(c)], s_x.at[stage, block(c)], x_save.at[c])

    def keeps(layer, kind, c):
        here = block(c)
        if kind == 0:
            pairs = [(gu.at[:, here], s_gu.at[layer, :, here]), (hid.at[here], s_hid.at[layer, here])]
        else:
            pairs = [(qkv.at[:, here], s_qkv.at[layer, :, here]), (att.at[here], s_att.at[layer, here])]
        return [pltpu.make_async_copy(a, b, keep_sem.at[kind, n, c]) for n, (a, b) in enumerate(pairs)]

    def activations(layer, kind):
        if kind == 0:
            pairs = [(s_gu.at[layer], gu), (s_hid.at[layer], hid)]
        else:
            pairs = [(s_qkv.at[layer], qkv), (s_att.at[layer], att)]
        return [pltpu.make_async_copy(a, b, act_sem.at[kind, n]) for n, (a, b) in enumerate(pairs)]

    def project(*pairs):
        def write(i):
            here = flow.slot(i)
            for at, wide in tiles(width, 1024):
                part = sum(dot_nt(right[at : at + wide, :], left()) for left, right in pairs)
                flow.running[here, at : at + wide] = part.T.astype(BF16)

        return write

    def by_extent(c, work):
        early = steps // 2

        @when(c < early)
        def _():
            work(early * big)

        @when(c >= early)
        def _():
            work(tokens)

    def normed_rows(stage, c):
        here = block(c)

        @when(stage > 0)
        def _():
            save_x(stage, c).wait()
            res[here, :] += flow.from_inner[flow.slot(c), :].astype(F32)

        save_x(stage, c).start()
        xhat, _ = standardize(res[here, :])
        low[...] = (xhat * norms[pl.ds(2 * stage, 1), :] + norms[pl.ds(2 * stage + 1, 1), :]).astype(BF16)
        pltpu.make_async_copy(low, s_n.at[stage, here], low_sem.at[0]).start()

    def attention_forward(t, layer, c):
        here = block(c)

        @when(layer > 0)
        def _():
            for copy in keeps(layer - 1, 1, c):
                copy.wait()

        for part in range(3):
            for at, wide in tiles(local):
                mixed = dot(low[...], w_attn[part, :, at : at + wide])
                for pair in range(wide // PAIR):
                    to_lane = at + pair * PAIR
                    span_here = slice(to_lane, to_lane + PAIR)
                    value = mixed[:, pair * PAIR : (pair + 1) * PAIR]
                    value = value + biases[pl.ds(3 * layer + part, 1), :][:, span_here]
                    if part < 2:
                        value = turn(value, [rope[n, here, :] for n in range(3)], 1.0)
                    qkv[part, here, span_here] = value.astype(BF16)
        def attend(keys):
            open_here = mask[c, 0:keys].astype(F32) > 0.0
            for pair in range(local // PAIR):
                lane = slice(pair * PAIR, (pair + 1) * PAIR)
                query, key, value = qkv[0, here, lane], qkv[1, 0:keys, lane], qkv[2, 0:keys, lane]
                outs = []
                for head in range(2):
                    own = first_head if head == 0 else jnp.logical_not(first_head)
                    scores = dot_nt(key, jnp.where(own, query, jnp.zeros_like(query))) * scale
                    scores = jnp.where(open_here, scores, -1e30)
                    exps = jnp.exp(scores - jnp.max(scores, axis=0, keepdims=True))
                    probs = exps * (1.0 / jnp.sum(exps, axis=0, keepdims=True))
                    outs.append(dot_tn(probs.astype(BF16), value))
                att[here, lane] = jnp.where(first_head, outs[0], outs[1]).astype(BF16)

        by_extent(c, attend)

        @when(layer < top)
        def _():
            for copy in keeps(layer, 1, c):
                copy.start()

        run_events(t, 1)
        project((lambda: att[here, :], w_attn.at[3]))(c)

    def ffn_forward(t, layer, c):
        here = block(c)

        @when(layer > 0)
        def _():
            for copy in keeps(layer - 1, 0, c):
                copy.wait()

        for at, wide in tiles(ff):
            gate = dot(low[...], w_ffn[0, :, at : at + wide])
            up = dot(low[...], w_ffn[1, :, at : at + wide])
            gu[0, here, at : at + wide] = gate.astype(BF16)
            gu[1, here, at : at + wide] = up.astype(BF16)
            hid[here, at : at + wide] = (gate * jax.nn.sigmoid(gate) * up).astype(BF16)

        @when(layer < top)
        def _():
            for copy in keeps(layer, 0, c):
                copy.start()

        run_events(t, 1)
        project((lambda: hid[here, :], w_ffn.at[2]))(c)

    def fetch_x(back, c):
        return pltpu.make_async_copy(s_x.at[half - back, block(c)], x_in, x_sem.at[0])

    def fetch_low(c):
        return pltpu.make_async_copy(s_y.at[0, block(c)], low, low_sem.at[1])

    def save_low(back, c):
        return pltpu.make_async_copy(low, s_y.at[back, block(c)], low_sem.at[0])

    def take(back, i, c):
        here = block(c)
        row = 2 * (half - back)
        fetch_x(back, c).wait()

        @when(back == 1)
        def _():
            fetch_low(c).wait()
            res[here, :] = low[...].astype(F32)

        xhat, rstd = standardize(x_in[...])
        e = flow.from_inner[flow.slot(i), :].astype(F32)
        scaled = e * norms[pl.ds(row, 1), :]
        inner = jnp.mean(scaled * xhat, axis=-1, keepdims=True)
        res[here, :] += rstd * (scaled - jnp.mean(scaled, axis=-1, keepdims=True) - xhat * inner)
        norm_acc[pl.ds(row, 1), :] += jnp.sum(e * xhat, axis=0, keepdims=True)
        norm_acc[pl.ds(row + 1, 1), :] += jnp.sum(e, axis=0, keepdims=True)

    def ffn_backward(i, c):
        here = block(c)
        for at, wide in tiles(ff):
            lane = slice(at, at + wide)
            d_hidden = dot(low[...], w_ffn[2, :, lane])
            gate, up = gu[0, here, lane].astype(F32), gu[1, here, lane].astype(F32)
            sigma = jax.nn.sigmoid(gate)
            gu[0, here, lane] = (d_hidden * up * sigma * (1.0 + gate * (1.0 - sigma))).astype(BF16)
            gu[1, here, lane] = (d_hidden * gate * sigma).astype(BF16)
        project((lambda: gu[0, here, :], w_ffn.at[0]), (lambda: gu[1, here, :], w_ffn.at[1]))(i)

    def attention_backward(layer, i, c):
        here = block(c)
        def attend_back(keys):
            open_here = mask[c, 0:keys].astype(F32) > 0.0
            turns = [rope[n, here, :] for n in range(3)]
            for pair in range(local // PAIR):
                lane = slice(pair * PAIR, (pair + 1) * PAIR)
                d_att = dot(low[...], w_attn[3, :, lane]).astype(BF16)
                query, key, value = qkv[0, here, lane], qkv[1, 0:keys, lane], qkv[2, 0:keys, lane]
                d_query = []
                for head in range(2):
                    own = first_head if head == 0 else jnp.logical_not(first_head)
                    own_query = jnp.where(own, query, jnp.zeros_like(query))
                    own_d_att = jnp.where(own, d_att, jnp.zeros_like(d_att))
                    scores = jnp.where(open_here, dot_nt(key, own_query) * scale, -1e30)
                    exps = jnp.exp(scores - jnp.max(scores, axis=0, keepdims=True))
                    probs = exps * (1.0 / jnp.sum(exps, axis=0, keepdims=True))
                    d_probs = dot_nt(value, own_d_att)
                    d_scores = probs * (d_probs - jnp.sum(probs * d_probs, axis=0, keepdims=True))
                    d_scores = d_scores.astype(BF16)
                    d_value[0:keys, lane] += dot(probs.astype(BF16), own_d_att)
                    d_key[0:keys, lane] += dot(d_scores, own_query)
                    d_query.append(dot_tn(d_scores, key))
                parts = [
                    turn(jnp.where(first_head, d_query[0], d_query[1]) * scale, turns, -1.0),
                    turn(d_key[here, lane] * scale, turns, -1.0),
                    d_value[here, lane],
                ]
                for part, values in enumerate(parts):
                    values = values.astype(BF16)
                    qkv[part, here, lane] = values
                    bias_acc[layer, part : part + 1, lane] += jnp.sum(values.astype(F32), axis=0, keepdims=True)

        by_extent(c, attend_back)
        project(
            (lambda: qkv[0, here, :], w_attn.at[0]),
            (lambda: qkv[1, here, :], w_attn.at[1]),
            (lambda: qkv[2, here, :], w_attn.at[2]),
        )(i)

    class Blocks:
        def __init__(self, back, kind):
            self.back_stage, self.kind = back, kind
            layer = top - back // 2
            self.sums = (sums_ffn if kind == 0 else sums_attn).at[layer]
            self.mate = (mate_ffn if kind == 0 else mate_attn).at[layer]
            self.via = (via_ffn if kind == 0 else via_attn).at[layer]
            self.home = 0 if group.square else group.chip
            self.stride = lane_stride(ff if kind == 0 else local)
            self.held = staged.at[:, :, 0 : (4 - (kind == 0)) * self.stride]
            self.x = s_n.at[2 * layer + 1 - kind]
            self.y = s_y.at[back]
            if kind == 0:
                self.right = [(0, gu.at[0]), (0, gu.at[1]), (1, hid)]
            else:
                self.right = [(0, qkv.at[0]), (0, qkv.at[1]), (0, qkv.at[2]), (1, att)]

        def chip(self, u):
            if not group.square:
                return (group.chip + 1 + u) % chips
            x, y, far = group.x // 2, group.y // 2, group.far // 2
            k = u % 4
            return jnp.where(k == 0, far, jnp.where(k == 1, x, jnp.where(k == 2, y, group.chip)))

        def fetch(self, u):
            core = jnp.where(u < chips, 1 - group.core, group.core)
            at = pl.multiple_of((self.chip(u) * 2 + core) * depth, depth)
            return [
                pltpu.make_async_copy(
                    source.at[:, pl.ds(at, depth)], columns.at[u % 2, n], column_sem.at[self.kind, u % 2, n]
                )
                for n, source in enumerate((self.x, self.y))
            ]

        def over(self, u):
            j = self.chip(u)
            sems = (mate_send.at[self.back_stage, j], mate_got.at[self.back_stage, j])
            return self.held.at[u % 2], self.mate.at[j], lambda a, b: to(a, b, *sems, {"fsdp": group.peer})

        def near(self, source, target, u):
            return source, target, lambda a, b: pltpu.make_async_copy(a, b, stage_sem.at[self.kind, u % 2])

        def bring(self, u):
            return self.near(self.mate.at[self.chip(u)], self.held.at[u % 2], u)

        def back(self, u):
            return self.near(self.held.at[u % 2], self.mate.at[self.chip(u)], u)

        def keep(self, u):
            return self.near(self.held.at[u % 2], self.sums.at[self.home], u)

        def push(self, u):
            j = self.chip(u)
            sems = (own_send.at[self.back_stage, j], own_got.at[self.back_stage, group.chip])
            return self.mate.at[j], self.sums.at[group.chip], lambda a, b: to(a, b, *sems, {"fsdp": group.at(j)})

        def hop(self, kind):
            over_x = kind % 2 == 0
            first = over_x if kind < 4 else not over_x
            rows = pl.ds(0 if first else depth // 2, depth // 2)
            target = group.x if over_x else group.y
            sems = (own_send.at[self.back_stage, kind], own_got.at[self.back_stage, kind])
            build = lambda a, b: to(a, b, *sems, {"fsdp": target})
            if kind < 2:
                return self.mate.at[group.far // 2, rows], self.via.at[kind], build
            place = self.sums.at[1 if over_x else 2, rows]
            if kind < 4:
                return self.mate.at[target // 2, rows], place, build
            return self.via.at[1 if over_x else 0], place, build

        def send_on(self, u):
            whole(*self.back(u)).wait()
            if not group.square:
                start(*self.push(u))
                return
            for k, hops in enumerate(((0, 1), (2,), (3,))):

                @when(u % 4 == k)
                def _(hops=hops):
                    for kind in hops:
                        start(*self.hop(kind))

        def relay(self):
            if not group.square:
                return
            rest = depth // 2
            steps_in = []
            for n, (kind, target, rows) in enumerate(
                ((1, group.x, pl.ds(rest, rest)), (0, group.y, pl.ds(0, rest)))
            ):
                whole(*self.hop(kind)).wait_recv()
                pair = [
                    pltpu.make_async_copy(self.mate.at[target // 2, rows], self.held.at[n, pl.ds(0, rest)], relay_sem.at[n, 0]),
                    pltpu.make_async_copy(self.via.at[kind], self.held.at[n, pl.ds(rest, rest)], relay_sem.at[n, 1]),
                ]
                for copy in pair:
                    copy.start()
                steps_in.append((kind, pair))
            returns = []
            lanes_here = (4 - (self.kind == 0)) * self.stride
            for n, (kind, pair) in enumerate(steps_in):
                for copy in pair:
                    copy.wait()
                for at, wide in tiles(lanes_here, 512):
                    lane = slice(at, at + wide)
                    both = staged[n, 0:rest, lane].astype(F32) + staged[n, rest:depth, lane].astype(F32)
                    staged[n, 0:rest, lane] = both.astype(BF16)
                copy = pltpu.make_async_copy(self.held.at[n, pl.ds(0, rest)], self.via.at[kind], relay_sem.at[n, 0])
                copy.start()
                returns.append(copy)
            for copy, kind in zip(returns, (4, 5)):
                copy.wait()
                start(*self.hop(kind))

        def unit(self, u):
            slot = u % 2
            own = u >= chips

            @when(u + 1 < units)
            def _():
                for copy in self.fetch(u + 1):
                    copy.start()

            @when((u >= 2) & (u < chips + 2))
            def _():
                whole(*self.over(u - 2)).wait_send()

            @when(u > chips)
            def _():
                self.send_on(u - 1)

            @when(own)
            def _():
                whole(*self.over(u - chips)).wait_recv()
                start(*self.bring(u))

            for copy in self.fetch(u):
                copy.wait()
            for left in range(2):
                turned[left] = columns[slot, left].T

            @when(own)
            def _():
                whole(*self.bring(u)).wait()

            for m, (left, right) in enumerate(self.right):
                for at, wide in tiles(right.shape[1]):
                    product = dot(turned[left], right[:, at : at + wide])
                    lane = slice(m * self.stride + at, m * self.stride + at + wide)
                    before = staged[slot, :, lane].astype(F32)
                    staged[slot, :, lane] = (product + jnp.where(own, before, 0.0)).astype(BF16)

            @when(jnp.logical_not(own))
            def _():
                start(*self.over(u))

            @when(own & (u < units - 1))
            def _():
                start(*self.back(u))

            @when(u == units - 1)
            def _():
                start(*self.keep(u))

        def begin(self):
            for copy in self.fetch(0):
                copy.start()

        def run(self, i):
            def one(r, carry):
                u = i * per_step + r

                @when(u < units)
                def _():
                    self.unit(u)

                return carry

            lax.fori_loop(0, per_step, one, 0)

        def end(self):
            whole(*self.keep(units - 1)).wait()

        def finish(self):
            if group.square:
                for kind in range(6):
                    whole(*self.hop(kind)).wait_send()
                    if kind >= 2:
                        whole(*self.hop(kind)).wait_recv()
                return
            for j in range(chips):

                @when(j != group.chip)
                def _(j=j):
                    sems = (own_send.at[self.back_stage, j], own_got.at[self.back_stage, j])
                    copy = to(self.mate.at[j], self.sums.at[j], *sems, {"fsdp": group.at(j)})
                    copy.wait_send()
                    copy.wait_recv()

    def save_out(c):
        return pltpu.make_async_copy(flow.running.at[flow.slot(c)], out_states.at[block(c)], out_sem.at[c])

    def save_grad(c):
        return pltpu.make_async_copy(res.at[block(c)], grad_states.at[block(c)], out_sem.at[c])

    def step(t, carry):
        i = t % steps
        stage = t // steps
        back = stage - half
        c = jnp.where(back < 0, i, steps - 1 - i)
        run_events(t, 0)

        @when((t >= steps) & (back < 0))
        def _():
            normed_rows(stage, c)
            flow.release(i, True)

        @when(t < steps)
        def _():
            normed_rows(stage, c)

        @when(back == 0)
        def _():
            save_x(half - 1, i).wait()

        @when((i == 0) & (back >= 1) & (back < half))
        def _():
            for k in range(2):

                @when(back % 2 == k)
                def _(k=k):
                    layer = top - back // 2

                    @when(back >= 2)
                    def _():
                        for kind in (2, 3) if k == 0 else (0, 1):
                            load(layer, kind, True)
                        for copy in activations(layer, k):
                            copy.wait()

                    @when(back + 1 < half)
                    def _():
                        for kind in (0, 1) if k == 0 else (2, 3):
                            load(layer - k, kind, False)

                    if k == 1:
                        d_key[...] = jnp.zeros_like(d_key)
                        d_value[...] = jnp.zeros_like(d_value)

        for k in range(2):

            @when((i == 0) & (back >= 1) & (back % 2 != k))
            def _(k=k):
                Blocks(back - 1, k).begin()

        @when(back >= 1)
        def _():
            take(back, i, c)
            flow.release(i, t < total)

        @when((t >= total - half * steps + steps - 1) & (t < total + steps - 1))
        def _():
            after = t + 1
            fetch_x(after // steps - half, steps - 1 - after % steps).start()

        @when((back >= 1) & (back < half))
        def _():
            low[...] = res[block(c), :].astype(BF16)
            save_low(back, c).start()

        @when(back == half)
        def _():
            save_grad(c).start()

        @when((t >= steps) & (t < total))
        def _():
            flow.clear(i)

        @when(back == 0)
        def _():
            out = res[block(i), :] + flow.from_inner[flow.slot(i), :].astype(F32)
            flow.release(i, True)
            flow.running[flow.slot(i), :] = out.astype(BF16)
            save_out(i).start()
            fetch_low(c).wait()
            save_out(i).wait()

        @when((back < 0) & (stage % 2 == 0))
        def _():
            attention_forward(t, stage // 2, c)

        @when((back < 0) & (stage % 2 == 1))
        def _():
            ffn_forward(t, stage // 2, c)

        @when((back >= 0) & (back < half) & (back % 2 == 0))
        def _():
            ffn_backward(i, c)

        @when((back >= 0) & (back < half) & (back % 2 == 1))
        def _():
            attention_backward(top - back // 2, i, c)

        @when(t < total)
        def _():
            flow.push(i, t >= steps)

        run_events(t, 2)

        @when((t < total) & (back != 0))
        def _():
            save_low(0, c).wait()

        after = t + 1
        @when((after >= half * steps) & (after < (half + 2) * steps))
        def _():
            fetch_low(steps - 1 - after % steps).start()

        for k in range(2):

            @when((back >= 1) & (back % 2 != k))
            def _(k=k):
                blocks = Blocks(back - 1, k)
                blocks.run(i)

                @when(i == steps - 1)
                def _():
                    blocks.end()
                    blocks.relay()

                    @when((back + 1 < half) & (back + 1 >= 2))
                    def _():
                        for copy in activations(top - (back + 1) // 2, k):
                            copy.start()

        k = t - flow.lag

        @when((k >= 0) & (k < total))
        def _():
            flow.pull((k + steps) % steps)

        return carry

    lax.fori_loop(0, total + steps, step, 0)

    for copy in small:
        copy.wait_send()
    parts = []
    for n, other in enumerate(group.everyone):
        at = pl.multiple_of(other * depth, depth)
        sems = (small_send.at[0, n], small_got.at[0, n])
        parts.append(to(norm_acc.at[:, pl.ds(at, depth)], norm_parts.at[shards - 1 - n], *sems, {"fsdp": other}))
        sems = (small_send.at[1, n], small_got.at[1, n])
        parts.append(to(bias_acc, bias_parts.at[shards - 1 - n], *sems, {"fsdp": other}))
    for copy in parts:
        copy.start()
    own = [
        pltpu.make_async_copy(norm_acc.at[:, mine], norm_parts.at[0], misc.at[0]),
        pltpu.make_async_copy(bias_acc, bias_parts.at[0], misc.at[1]),
    ]
    for copy in own:
        copy.start()
    for copy in own:
        copy.wait()
    for i in range(steps):
        save_grad(i).wait()
        flow.clear(i)
    for layer in range(LAYERS):
        for kind in range(4):
            gather(layer, kind).finish()
    for copy in parts:
        copy.wait_send()
        copy.wait_recv()
    for back in range(half):
        Blocks(back, back % 2).finish()


def lane_stride(extent):
    return -(-extent // PAIR) * PAIR


def plan(tokens):
    return next((s, p) for s, p in ((6, 1), (3, 1), (2, 1)) if tokens % (16 * s * p) == 0)


def train(states, cotangent, own_norms, own_bias, rope, mask, own_q, own_o, own_g, own_d):
    count, shards = lax.axis_size("tensor"), lax.axis_size("fsdp")
    tokens, width = states.shape
    steps, span = plan(tokens)
    big = tokens // steps
    chips = shards // 2
    depth = width // shards
    local, ff = own_q.shape[-1], own_g.shape[-1]
    lanes_attn, lanes_ffn = 4 * lane_stride(local), 3 * lane_stride(ff)
    parts = 3 if chips == 4 else chips
    per_step = -(-2 * chips // max(steps - 2, 1))
    shape = jax.ShapeDtypeStruct
    outs = [
        shape((tokens, width), BF16),
        shape((tokens, width), F32),
        shape((LAYERS, parts, depth, lanes_attn), BF16),
        shape((LAYERS, parts, depth, lanes_ffn), BF16),
        shape((shards, 4 * LAYERS, depth), F32),
        shape((shards, LAYERS, 8, local), F32),
        *[shape((LAYERS, shards) + own.shape[1:], BF16) for own in (own_q, own_o, own_g, own_d)],
        shape((2 * LAYERS, tokens, width), F32),
        shape((2 * LAYERS, tokens, width), BF16),
        shape((2 * LAYERS, tokens, width), BF16),
        shape((LAYERS - 1, 3, tokens, local), BF16),
        shape((LAYERS - 1, tokens, local), BF16),
        shape((LAYERS - 1, 2, tokens, ff), BF16),
        shape((LAYERS - 1, tokens, ff), BF16),
        shape((LAYERS, chips, depth, lanes_attn), BF16),
        shape((LAYERS, chips, depth, lanes_ffn), BF16),
        shape((LAYERS, 2, depth // 2, lanes_attn), BF16),
        shape((LAYERS, 2, depth // 2, lanes_ffn), BF16),
    ]
    dma = pltpu.SemaphoreType.DMA
    vmem = pltpu.VMEM
    scratch = [
        vmem((tokens, width), F32),
        vmem((4, width, local), BF16),
        vmem((3, width, ff), BF16),
        vmem((2, tokens, ff), BF16),
        vmem((tokens, ff), BF16),
        vmem((3, tokens, local), BF16),
        vmem((tokens, local), BF16),
        vmem((tokens, local), F32),
        vmem((tokens, local), F32),
        vmem((big, width), F32),
        vmem((big, width), BF16),
        vmem((4 * LAYERS, width), F32),
        vmem((8, local), F32),
        vmem((shards, 8, PAIR), F32),
        vmem((4 * LAYERS, width), F32),
        vmem((LAYERS, 8, local), F32),
        vmem((2, 2, tokens, depth), BF16),
        vmem((2, depth, tokens), BF16),
        vmem((2, depth, max(lanes_attn, lanes_ffn)), BF16),
        dma((steps,)),
        dma((1,)),
        dma((2,)),
        dma((steps,)),
        dma((2, 2, steps)),
        dma((2, 2)),
        dma((4,)),
        dma((4, shards)),
        dma((4 * LAYERS, gather_kinds(shards))),
        dma((4 * LAYERS, gather_kinds(shards))),
        dma((2, 2, 2)),
        dma((2, 2)),
        dma((2, 2)),
        *([dma((2 * LAYERS, max(chips, 6)))] * 4),
        dma((2, shards)),
        dma((2, shards)),
        *flow_scratch(steps, span, tokens, width),
    ]
    flops = 6 * LAYERS * tokens * width * (4 * local + 3 * ff)
    return pl.pallas_call(
        functools.partial(train_kernel, count, shards, steps, span, per_step),
        out_shape=outs,
        in_specs=[ANY, ANY, VMEM, VMEM, VMEM, VMEM, ANY, ANY, ANY, ANY],
        out_specs=[ANY] * len(outs),
        scratch_shapes=scratch,
        compiler_params=pltpu.CompilerParams(
            collective_id=1, has_side_effects=True, vmem_limit_bytes=64 * 1024 * 1024
        ),
        cost_estimate=pl.CostEstimate(flops=flops, bytes_accessed=flops // 256, transcendentals=0),
        name="train",
    )(states, cotangent, own_norms, own_bias, rope, mask, own_q, own_o, own_g, own_d)


def finish_kernel(attn, ffn, states, grads, g_qkv, g_out, g_gate_up, g_down, out_states, out_grads):
    local, ff = g_qkv.shape[3], g_gate_up.shape[3]

    def total(parts, at, wide):
        return sum(parts[0, n, :, at : at + wide].astype(F32) for n in range(parts.shape[1]))

    for m in range(3):
        g_qkv[0, m] = total(attn, m * lane_stride(local), local)
    g_out[0] = total(attn, 3 * lane_stride(local), local).T
    for m in range(2):
        g_gate_up[0, :, m, :] = total(ffn, m * lane_stride(ff), ff)
    g_down[0] = total(ffn, 2 * lane_stride(ff), ff).T
    out_states[...] = states[...]
    out_grads[...] = grads[...]


def finish(sums_attn, sums_ffn, states, grads, local, ff):
    parts, depth = sums_attn.shape[1:3]
    tokens, width = states.shape
    rows = min(PAIR, depth)
    cuts = depth // rows
    pieces = tokens // (LAYERS * cuts)
    shape = jax.ShapeDtypeStruct
    spec = pl.BlockSpec
    token_spec = spec((pieces, width), lambda l, r: (l * cuts + r, 0))
    return pl.pallas_call(
        finish_kernel,
        grid=(LAYERS, cuts),
        in_specs=[
            spec((1, parts, rows, sums_attn.shape[3]), lambda l, r: (l, 0, r, 0)),
            spec((1, parts, rows, sums_ffn.shape[3]), lambda l, r: (l, 0, r, 0)),
            token_spec,
            token_spec,
        ],
        out_specs=[
            spec((1, 3, rows, local), lambda l, r: (l, 0, r, 0)),
            spec((1, local, rows), lambda l, r: (l, 0, r)),
            spec((1, rows, 2, ff), lambda l, r: (l, r, 0, 0)),
            spec((1, ff, rows), lambda l, r: (l, 0, r)),
            token_spec,
            token_spec,
        ],
        out_shape=[
            shape((LAYERS, 3, depth, local), F32),
            shape((LAYERS, local, depth), F32),
            shape((LAYERS, depth, 2, ff), F32),
            shape((LAYERS, ff, depth), F32),
            shape((tokens, width), BF16),
            shape((tokens, width), F32),
        ],
        compiler_params=pltpu.CompilerParams(vmem_limit_bytes=48 * 1024 * 1024),
        name="finish",
    )(sums_attn, sums_ffn, states, grads)


def tables(segment_ids, rows):
    places = jnp.arange(rows, dtype=jnp.int32)
    previous = jnp.concatenate([segment_ids[:1] - 1, segment_ids[:-1]])
    starts = lax.cummax(jnp.where(segment_ids != previous, places, jnp.zeros_like(places)), axis=0)
    position = places - starts
    half = ROT_DIM // 2
    inverse = rotary_base ** (-(jnp.arange(half, dtype=F32) * 2.0 / ROT_DIM))
    angle = position.astype(F32)[:, None] * inverse[None, :]
    cosine, sine = jnp.cos(angle), jnp.sin(angle)
    rest = jnp.zeros((rows, HEAD_DIM - ROT_DIM), F32)
    none = jnp.zeros_like(sine)
    rope = jnp.stack(
        [
            jnp.tile(jnp.concatenate([cosine, cosine, rest + 1.0], axis=1), (1, 2)),
            jnp.tile(jnp.concatenate([-sine, none, rest], axis=1), (1, 2)),
            jnp.tile(jnp.concatenate([none, sine, rest], axis=1), (1, 2)),
        ]
    )
    allowed = (segment_ids[:, None] == segment_ids[None, :]) & (places[None, :] <= places[:, None])
    return rope, allowed.astype(F32)


def on_device(
    states,
    segment_ids,
    ln1_gain,
    ln1_bias,
    qkv_weight,
    qkv_bias,
    out_weight,
    ln2_gain,
    ln2_bias,
    gate_up_weight,
    down_weight,
    cotangent,
):
    tokens = states.shape[0]
    rope, allowed = tables(segment_ids, tokens)
    steps = plan(tokens)[0]
    mask = allowed.reshape(steps, -1, tokens).transpose(0, 2, 1).astype(BF16)
    own_norms = jnp.stack([ln1_gain, ln1_bias, ln2_gain, ln2_bias], axis=1).reshape(4 * LAYERS, -1).astype(F32)
    own_bias = qkv_bias.reshape(LAYERS * 3, -1).astype(F32)
    own_bias = jnp.pad(own_bias, ((0, 8 - own_bias.shape[0]), (0, PAIR - own_bias.shape[1])))
    out_states, grad_states, sums_attn, sums_ffn, norm_parts, bias_parts, *_ = train(
        states,
        cotangent,
        own_norms,
        own_bias,
        rope,
        mask,
        qkv_weight.transpose(0, 2, 1, 3),
        out_weight.transpose(0, 2, 1)[:, None],
        gate_up_weight.transpose(0, 2, 1, 3),
        down_weight.transpose(0, 2, 1)[:, None],
    )
    g_qkv, g_out, g_gate_up, g_down, out_states, grad_states = finish(
        sums_attn, sums_ffn, out_states, grad_states, qkv_weight.shape[3], gate_up_weight.shape[3]
    )
    g_norms = jnp.sum(norm_parts, axis=0).reshape(LAYERS, 4, -1)
    g_bias = jnp.sum(bias_parts, axis=0).reshape(LAYERS, 8, -1, HEAD_DIM)[:, :3]
    share = qkv_bias.shape[3]
    g_bias = lax.dynamic_slice_in_dim(g_bias, lax.axis_index("fsdp") * share, share, axis=3)
    return (
        out_states,
        grad_states,
        g_norms[:, 0],
        g_norms[:, 1],
        g_qkv.transpose(0, 2, 1, 3),
        g_bias,
        g_out,
        g_norms[:, 2],
        g_norms[:, 3],
        g_gate_up,
        g_down,
    )


def solution(mesh):
    in_specs = (
        P("fsdp", None),
        P("fsdp"),
        P(None, "fsdp"),
        P(None, "fsdp"),
        P(None, "fsdp", None, "tensor"),
        P(None, None, "tensor", "fsdp"),
        P(None, "tensor", "fsdp"),
        P(None, "fsdp"),
        P(None, "fsdp"),
        P(None, "fsdp", None, "tensor"),
        P(None, "tensor", "fsdp"),
        P("fsdp", None),
    )
    out_specs = (
        P("fsdp", None),
        P("fsdp", None),
        P(None, "fsdp"),
        P(None, "fsdp"),
        P(None, "fsdp", None, "tensor"),
        P(None, None, "tensor", "fsdp"),
        P(None, "tensor", "fsdp"),
        P(None, "fsdp"),
        P(None, "fsdp"),
        P(None, "fsdp", None, "tensor"),
        P(None, "tensor", "fsdp"),
    )
    return jax.shard_map(
        on_device, mesh=mesh, in_specs=in_specs, out_specs=out_specs, check_vma=False
    )
```

time: 1810 us -> 740 us (0.41)
  waiting for transfers between devices: 1210 us -> 0 us
  Pallas kernels: 0 us -> 714 us
  matrix products: 246 us -> 0 us
  blocking collectives: 110 us -> 0 us
  other arithmetic: 107 us -> 6.12 us
  local copies, waits for them, and re-layouts: 108 us -> 16.4 us
    pallas_call x0 -> x2, Pallas kernels: none -> 714 us  [the longest x1 699 us: train(): pl.pallas_call(functools.partial(train_kernel, count, shards, steps, span...]
    psum x7 -> x0, waiting for transfers between devices: 606 us -> none  [the longest x2 187 us: forward_layer(): lax.psum(ff_part.astype(jnp.bfloat16), 'tensor').astype(jnp.float32)]
    reduce_scatter x8 -> x0, waiting for transfers between devices: 388 us -> none  [the longest x2 177 us: backward_layer(): lax.psum_scatter(g_gate_up.astype(jnp.bfloat16), 'fsdp', scatter_dimensio...]
    dot_general x36 -> x0, matrix products: 246 us -> none  [the longest x2 30.4 us: backward_layer(): jnp.einsum('td,tcf->dcf', second_normalized_rows, d_gate_up, preferred_el...]
    all_gather x8 -> x0, waiting for transfers between devices: 219 us -> none  [the longest x2 114 us: fetch_forward(): lax.all_gather(gate_up_w, 'fsdp', axis=0, tiled=True)]
    all_gather x10 -> x0, blocking collectives: 87.5 us -> none  [the longest x2 18.4 us: fetch_forward(): lax.all_gather(qkv_b, 'fsdp', axis=2, tiled=True)]
    reduce_sum x20 -> x2, other arithmetic: 46.2 us -> 0.03 us  [the longest x1 0.02 us: on_device(): g_bias = jnp.sum(bias_parts, axis=0).reshape(LAYERS, 8, -1, HEAD_DIM)[:, :3]]
    unnamed x238 -> x29, local copies, waits for them, and re-layouts: 44.1 us -> 9.53 us
  transfers between devices with their start and end apart: 23 -> 0, of which waited for: 21 -> 0; matrix products, arithmetic and copies ran while one was open for 17% -> 0% of each run, Pallas kernels for 0% -> 0%
where the time goes in v1:
time: 740 us; the launch traced here: 738 us
  Pallas kernels  714 us (96%)
  local copies, waits for them, and re-layouts  16.4 us (2%)
    pallas_call x1, Pallas kernels, train(): pl.pallas_call(functools.partial(train_kernel, count, shards, steps, span...  699 us
    pallas_call x1, Pallas kernels, finish(): pl.pallas_call(finish_kernel, grid=(LAYERS, cuts), in_specs=[spec((1, par...  15.4 us

profile of v1, /device:TPU:17, one launch (start us, length us, event | category | flops | bytes accessed | tf_op | source)
XLA Modules:
  0.0 738.4 jit_solution(10437624411073353295)
XLA Ops:
  0.6 1.2 slice.31
  2.5 0.8 iota_select_fusion
  3.3 0.3 reduce-window.9
  3.6 0.1 slice.33
  3.7 0.1 slice_reduce_fusion
  3.8 0.1 maximum_bitcast_fusion
  3.9 0.0 copy-start.1
  3.9 0.2 multiply_cosine_fusion
  4.1 0.1 pad.20.clone
  4.2 0.1 pad.23.clone
  4.3 0.8 maximum_maximum_fusion.1
  5.1 0.1 copy.44
  5.3 0.9 tile.26
  6.2 0.9 copy.45
  7.1 0.9 tile.28
  8.0 0.9 copy.46
  8.9 2.0 pad_maximum_fusion.rope
  10.9 0.0 copy-done.1
  10.9 1.9 copy.59
  12.8 0.0 copy-start.9
  12.8 0.0 copy-start.10
  12.9 0.0 copy-start.6
  12.9 2.6 copy.49
  15.5 0.0 copy-done.4
  15.5 0.1 eq.17
  15.5 1.2 convert_convert_fusion.mask
  16.8 0.0 copy-done.2
  16.8 1.0 copy.47
  17.8 0.0 copy-done.7
  17.8 0.0 copy-done.8
  17.8 0.0 copy-done.9
  17.8 0.0 copy-done.10
  17.9 0.6 reshape.102.own_norms
  18.5 0.0 copy-done.6
  18.5 0.1 convert_element_type.24
  18.6 0.6 pad_convert_fusion.own_bias
  19.2 699.0 %train.1 = (bf16[576,2048]{1,0:T(8,128)(2,1)}, f32[576,2048]{1,0:T(8,128)}, bf16[2,3,256,2048]{3,2,1,0:T(8,128)(2,1)}, bf16[2,3,256,4224]{3,2,1,0:T(8,128)(2,1)}...) custom-call(bf16[576,2048]{1,0:T(8,128)(2,1)} %states.1, ...), custom_call_target="tpu_custom_call" | custom-call | flops 88785027072 | bytes 346816512 | tf_op jit(solution)/shard_map/train/pallas_call | solution.py:1111
  718.2 0.0 copy-start
  718.2 1.7 copy-done
  719.8 15.4 %finish.1 = (f32[2,3,256,512]{3,2,1,0:T(8,128)}, f32[2,512,256]{2,1,0:T(8,128)}, f32[2,256,2,1408]{3,2,1,0:T(2,128)}, f32[2,1408,256]{2,1,0:T(8,128)}, bf16[576,2048]{1,0:T(8,128)(2,1)}, /*index=5*/f32[576,2048]{1,0:T(8,128)}) custom-call(bf16[2,3,256,2048]{3,2,1,0:T(8,128)(2,1)} %get-tuple-element.23.attn, bf16[2,3,256,4224]{3,2,1,0:T(8,128)(2,1)} %get-tuple-element.24.ffn, ...), custom_call_target="tpu_custom_call" | custom-call | tf_op jit(solution)/shard_map/finish/pallas_call | solution.py:1150
  735.2 0.0 copy-done.3
  735.3 0.1 reshape.101
  735.4 0.7 constant_dynamic-slice_fusion
  736.0 0.0 copy-done.5
  736.1 0.6 copy.60
  736.7 0.6 copy.61
  737.3 0.6 copy.62
  737.8 0.6 copy.63
  (25 shorter events, 0.2 us)
Async XLA Ops:
  3.9 7.0 copy-start.1
  12.8 2.6 copy-start.4
  12.8 3.9 copy-start.2
  12.8 4.9 copy-start.7
  12.8 5.0 copy-start.8
  12.8 5.0 copy-start.9
  12.8 5.0 copy-start.10
  12.9 5.6 copy-start.6
  718.2 1.7 copy-start
  719.8 15.4 %copy-start.3 = (f32[8,2,8,512]{3,2,1,0:T(8,128)S(1)}, f32[8,2,8,512]{3,2,1,0:T(8,128)}, u32[]{:S(2)}) copy-start(f32[8,2,8,512]{3,2,1,0:T(8,128)} %get-tuple-element.31) | copy-start | bytes 786436
  719.8 16.2 %copy-start.5 = (f32[8,8,256]{2,1,0:T(8,128)S(1)}, f32[8,8,256]{2,1,0:T(8,128)}, u32[]{:S(2)}) copy-start(f32[8,8,256]{2,1,0:T(8,128)} %get-tuple-element.29) | copy-start | bytes 196612

commit v2 on v1

--- a/solution.py
+++ b/solution.py
@@ -304,7 +304,7 @@
     whole_q, whole_o, whole_g, whole_d, s_x, s_n, s_y, s_qkv, s_att, s_gu, s_hid,
     mate_attn, mate_ffn, via_attn, via_ffn,
     res, w_attn, w_ffn, gu, hid, qkv, att, d_key, d_value, x_in, low,
-    norms, biases, bias_in, norm_acc, bias_acc, columns, turned, staged,
+    log_total, norms, biases, bias_in, norm_acc, bias_acc, columns, turned, staged,
     x_save, x_sem, low_sem, out_sem, keep_sem, act_sem, misc, load_sem, g_send, g_arrive,
     column_sem, stage_sem, relay_sem, mate_send, mate_got, own_send, own_got, small_send, small_got,
     *flow_refs,
@@ -317,7 +317,7 @@
     group = Group(shards)
     chips = group.chips
     flow = Flow(line, steps, span, big // span, flow_refs)
-    scale = 1.0 / math.sqrt(HEAD_DIM)
+    scale = jnp.asarray(1.0 / math.sqrt(HEAD_DIM), BF16)
     half = 2 * LAYERS
     stages = 2 * half
     total = stages * steps
@@ -525,17 +525,19 @@
                         value = turn(value, [rope[n, here, :] for n in range(3)], 1.0)
                     qkv[part, here, span_here] = value.astype(BF16)
         def attend(keys):
-            open_here = mask[c, 0:keys].astype(F32) > 0.0
+            closed = mask[c, 0:keys].astype(F32)
             for pair in range(local // PAIR):
                 lane = slice(pair * PAIR, (pair + 1) * PAIR)
-                query, key, value = qkv[0, here, lane], qkv[1, 0:keys, lane], qkv[2, 0:keys, lane]
+                query, key, value = qkv[0, here, lane] * scale, qkv[1, 0:keys, lane], qkv[2, 0:keys, lane]
                 outs = []
                 for head in range(2):
                     own = first_head if head == 0 else jnp.logical_not(first_head)
-                    scores = dot_nt(key, jnp.where(own, query, jnp.zeros_like(query))) * scale
-                    scores = jnp.where(open_here, scores, -1e30)
-                    exps = jnp.exp(scores - jnp.max(scores, axis=0, keepdims=True))
-                    probs = exps * (1.0 / jnp.sum(exps, axis=0, keepdims=True))
+                    scores = dot_nt(key, jnp.where(own, query, jnp.zeros_like(query))) + closed
+                    most = jnp.max(scores, axis=0, keepdims=True)
+                    exps = jnp.exp(scores - most)
+                    total_exp = jnp.sum(exps, axis=0, keepdims=True)
+                    log_total[layer, c, 2 * pair + head : 2 * pair + head + 1, :] = most + jnp.log(total_exp)
+                    probs = exps * (1.0 / total_exp)
                     outs.append(dot_tn(probs.astype(BF16), value))
                 att[here, lane] = jnp.where(first_head, outs[0], outs[1]).astype(BF16)
 
@@ -613,7 +615,7 @@
     def attention_backward(layer, i, c):
         here = block(c)
         def attend_back(keys):
-            open_here = mask[c, 0:keys].astype(F32) > 0.0
+            closed = mask[c, 0:keys].astype(F32)
             turns = [rope[n, here, :] for n in range(3)]
             for pair in range(local // PAIR):
                 lane = slice(pair * PAIR, (pair + 1) * PAIR)
@@ -622,11 +624,10 @@
                 d_query = []
                 for head in range(2):
                     own = first_head if head == 0 else jnp.logical_not(first_head)
-                    own_query = jnp.where(own, query, jnp.zeros_like(query))
+                    own_query = jnp.where(own, query, jnp.zeros_like(query)) * scale
                     own_d_att = jnp.where(own, d_att, jnp.zeros_like(d_att))
-                    scores = jnp.where(open_here, dot_nt(key, own_query) * scale, -1e30)
-                    exps = jnp.exp(scores - jnp.max(scores, axis=0, keepdims=True))
-                    probs = exps * (1.0 / jnp.sum(exps, axis=0, keepdims=True))
+                    scores = dot_nt(key, own_query) + closed
+                    probs = jnp.exp(scores - log_total[layer, c, 2 * pair + head : 2 * pair + head + 1, :])
                     d_probs = dot_nt(value, own_d_att)
                     d_scores = probs * (d_probs - jnp.sum(probs * d_probs, axis=0, keepdims=True))
                     d_scores = d_scores.astype(BF16)
@@ -634,8 +635,8 @@
                     d_key[0:keys, lane] += dot(d_scores, own_query)
                     d_query.append(dot_tn(d_scores, key))
                 parts = [
-                    turn(jnp.where(first_head, d_query[0], d_query[1]) * scale, turns, -1.0),
-                    turn(d_key[here, lane] * scale, turns, -1.0),
+                    turn(jnp.where(first_head, d_query[0], d_query[1]) / math.sqrt(HEAD_DIM), turns, -1.0),
+                    turn(d_key[here, lane], turns, -1.0),
                     d_value[here, lane],
                 ]
                 for part, values in enumerate(parts):
@@ -818,17 +819,12 @@
             for copy in self.fetch(0):
                 copy.start()
 
-        def run(self, i):
-            def one(r, carry):
-                u = i * per_step + r
-
-                @when(u < units)
-                def _():
-                    self.unit(u)
-
+        def run(self, first, last):
+            def one(u, carry):
+                self.unit(u)
                 return carry
 
-            lax.fori_loop(0, per_step, one, 0)
+            lax.fori_loop(first, last, one, 0)
 
         def end(self):
             whole(*self.keep(units - 1)).wait()
@@ -973,12 +969,17 @@
             @when((back >= 1) & (back % 2 != k))
             def _(k=k):
                 blocks = Blocks(back - 1, k)
-                blocks.run(i)
-
-                @when(i == steps - 1)
+                extra = back == half
+                pace = jnp.where(extra, 2 * per_step, per_step)
+                blocks.run(jnp.minimum(i * pace, units), jnp.minimum((i + 1) * pace, units))
+
+                @when(i == jnp.where(extra, min(3, steps - 1), steps - 1))
                 def _():
                     blocks.end()
                     blocks.relay()
+
+                @when(i == steps - 1)
+                def _():
 
                     @when((back + 1 < half) & (back + 1 >= 2))
                     def _():
@@ -1081,6 +1082,7 @@
         vmem((tokens, local), F32),
         vmem((big, width), F32),
         vmem((big, width), BF16),
+        vmem((LAYERS, steps, local // HEAD_DIM, big), F32),
         vmem((4 * LAYERS, width), F32),
         vmem((8, local), F32),
         vmem((shards, 8, PAIR), F32),
@@ -1196,7 +1198,7 @@
         ]
     )
     allowed = (segment_ids[:, None] == segment_ids[None, :]) & (places[None, :] <= places[:, None])
-    return rope, allowed.astype(F32)
+    return rope, jnp.where(allowed, 0.0, -1e30)
 
 
 def on_device(

time: 740 us -> 730 us (0.986)
  Pallas kernels: 714 us -> 704 us
    pallas_call x1, Pallas kernels: 699 us -> 689 us  [train(): pl.pallas_call(functools.partial(train_kernel, count, shards, steps, span...]
where the time goes in v2:
time: 730 us; the launch traced here: 728 us
  Pallas kernels  704 us (96%)
  local copies, waits for them, and re-layouts  16.4 us (2%)
    pallas_call x1, Pallas kernels, train(): pl.pallas_call(functools.partial(train_kernel, count, shards, steps, span...  689 us
    pallas_call x1, Pallas kernels, finish(): pl.pallas_call(finish_kernel, grid=(LAYERS, cuts), in_specs=[spec((1, par...  15.4 us

profile of v2, /device:TPU:17, one launch (start us, length us, event | category | flops | bytes accessed | tf_op | source)
XLA Modules:
  0.0 728.3 jit_solution(4971689451972835533)
XLA Ops:
  0.6 1.2 slice.31
  2.5 0.8 iota_select_fusion
  3.3 0.3 reduce-window.9
  3.6 0.1 slice.33
  3.7 0.1 slice_reduce_fusion
  3.8 0.1 maximum_bitcast_fusion
  3.9 0.0 copy-start.1
  3.9 0.2 multiply_cosine_fusion
  4.1 0.1 pad.20.clone
  4.2 0.1 pad.23.clone
  4.3 0.8 maximum_maximum_fusion.1
  5.1 0.1 copy.44
  5.3 0.9 tile.26
  6.2 0.9 copy.45
  7.1 0.9 tile.28
  8.0 0.9 copy.46
  8.9 2.0 pad_maximum_fusion.rope
  10.9 0.0 copy-done.1
  10.9 1.9 copy.59
  12.8 0.0 copy-start.9
  12.8 0.0 copy-start.10
  12.9 0.0 copy-start.6
  12.9 2.6 copy.49
  15.5 0.0 copy-done.4
  15.5 0.1 eq.17
  15.5 1.2 select_convert_fusion.mask
  16.8 0.0 copy-done.2
  16.8 1.0 copy.47
  17.8 0.0 copy-done.7
  17.8 0.0 copy-done.8
  17.8 0.0 copy-done.9
  17.8 0.0 copy-done.10
  17.9 0.6 reshape.102.own_norms
  18.5 0.0 copy-done.6
  18.5 0.1 convert_element_type.19
  18.6 0.6 pad_convert_fusion.own_bias
  19.2 688.9 %train.1 = (bf16[576,2048]{1,0:T(8,128)(2,1)}, f32[576,2048]{1,0:T(8,128)}, bf16[2,3,256,2048]{3,2,1,0:T(8,128)(2,1)}, bf16[2,3,256,4224]{3,2,1,0:T(8,128)(2,1)}...) custom-call(bf16[576,2048]{1,0:T(8,128)(2,1)} %states.1, ...), custom_call_target="tpu_custom_call" | custom-call | flops 88785027072 | bytes 346816512 | tf_op jit(solution)/shard_map/train/pallas_call | solution.py:1113
  708.1 0.0 copy-start
  708.1 1.7 copy-done
  709.8 15.4 %finish.1 = (f32[2,3,256,512]{3,2,1,0:T(8,128)}, f32[2,512,256]{2,1,0:T(8,128)}, f32[2,256,2,1408]{3,2,1,0:T(2,128)}, f32[2,1408,256]{2,1,0:T(8,128)}, bf16[576,2048]{1,0:T(8,128)(2,1)}, /*index=5*/f32[576,2048]{1,0:T(8,128)}) custom-call(bf16[2,3,256,2048]{3,2,1,0:T(8,128)(2,1)} %get-tuple-element.23.attn, bf16[2,3,256,4224]{3,2,1,0:T(8,128)(2,1)} %get-tuple-element.24.ffn, ...), custom_call_target="tpu_custom_call" | custom-call | tf_op jit(solution)/shard_map/finish/pallas_call | solution.py:1152
  725.2 0.0 copy-done.3
  725.2 0.1 reshape.101
  725.3 0.7 constant_dynamic-slice_fusion
  726.0 0.0 copy-done.5
  726.0 0.6 copy.60
  726.6 0.6 copy.61
  727.2 0.6 copy.62
  727.8 0.6 copy.63
  (25 shorter events, 0.2 us)
Async XLA Ops:
  3.9 7.0 copy-start.1
  12.8 2.6 copy-start.4
  12.8 4.0 copy-start.2
  12.8 5.0 copy-start.7
  12.8 5.0 copy-start.8
  12.8 5.0 copy-start.9
  12.8 5.0 copy-start.10
  12.9 5.6 copy-start.6
  708.1 1.7 copy-start
  709.8 15.4 %copy-start.3 = (f32[8,2,8,512]{3,2,1,0:T(8,128)S(1)}, f32[8,2,8,512]{3,2,1,0:T(8,128)}, u32[]{:S(2)}) copy-start(f32[8,2,8,512]{3,2,1,0:T(8,128)} %get-tuple-element.31) | copy-start | bytes 786436
  709.8 16.2 %copy-start.5 = (f32[8,8,256]{2,1,0:T(8,128)S(1)}, f32[8,8,256]{2,1,0:T(8,128)}, u32[]{:S(2)}) copy-start(f32[8,8,256]{2,1,0:T(8,128)} %get-tuple-element.29) | copy-start | bytes 196612

commit v3 on v2

--- a/solution.py
+++ b/solution.py
@@ -621,7 +621,7 @@
                 lane = slice(pair * PAIR, (pair + 1) * PAIR)
                 d_att = dot(low[...], w_attn[3, :, lane]).astype(BF16)
                 query, key, value = qkv[0, here, lane], qkv[1, 0:keys, lane], qkv[2, 0:keys, lane]
-                d_query = []
+                d_query, key_parts, value_parts = [], [], []
                 for head in range(2):
                     own = first_head if head == 0 else jnp.logical_not(first_head)
                     own_query = jnp.where(own, query, jnp.zeros_like(query)) * scale
@@ -631,9 +631,11 @@
                     d_probs = dot_nt(value, own_d_att)
                     d_scores = probs * (d_probs - jnp.sum(probs * d_probs, axis=0, keepdims=True))
                     d_scores = d_scores.astype(BF16)
-                    d_value[0:keys, lane] += dot(probs.astype(BF16), own_d_att)
-                    d_key[0:keys, lane] += dot(d_scores, own_query)
+                    key_parts.append(dot(d_scores, own_query))
+                    value_parts.append(dot(probs.astype(BF16), own_d_att))
                     d_query.append(dot_tn(d_scores, key))
+                d_key[0:keys, lane] += key_parts[0] + key_parts[1]
+                d_value[0:keys, lane] += value_parts[0] + value_parts[1]
                 parts = [
                     turn(jnp.where(first_head, d_query[0], d_query[1]) / math.sqrt(HEAD_DIM), turns, -1.0),
                     turn(d_key[here, lane], turns, -1.0),
@@ -796,12 +798,22 @@
             def _():
                 whole(*self.bring(u)).wait()
 
-            for m, (left, right) in enumerate(self.right):
-                for at, wide in tiles(right.shape[1]):
-                    product = dot(turned[left], right[:, at : at + wide])
-                    lane = slice(m * self.stride + at, m * self.stride + at + wide)
-                    before = staged[slot, :, lane].astype(F32)
-                    staged[slot, :, lane] = (product + jnp.where(own, before, 0.0)).astype(BF16)
+            def form(add):
+                for m, (left, right) in enumerate(self.right):
+                    for at, wide in tiles(right.shape[1]):
+                        product = dot(turned[left], right[:, at : at + wide])
+                        lane = slice(m * self.stride + at, m * self.stride + at + wide)
+                        if add:
+                            product = product + staged[slot, :, lane].astype(F32)
+                        staged[slot, :, lane] = product.astype(BF16)
+
+            @when(own)
+            def _():
+                form(True)
+
+            @when(jnp.logical_not(own))
+            def _():
+                form(False)
 
             @when(jnp.logical_not(own))
             def _():
@@ -1181,24 +1193,18 @@
 
 def tables(segment_ids, rows):
     places = jnp.arange(rows, dtype=jnp.int32)
-    previous = jnp.concatenate([segment_ids[:1] - 1, segment_ids[:-1]])
-    starts = lax.cummax(jnp.where(segment_ids != previous, places, jnp.zeros_like(places)), axis=0)
-    position = places - starts
+    same = segment_ids[:, None] == segment_ids[None, :]
+    earlier = places[None, :] < places[:, None]
+    position = jnp.sum(jnp.where(same & earlier, 1.0, 0.0), axis=1)
     half = ROT_DIM // 2
-    inverse = rotary_base ** (-(jnp.arange(half, dtype=F32) * 2.0 / ROT_DIM))
-    angle = position.astype(F32)[:, None] * inverse[None, :]
-    cosine, sine = jnp.cos(angle), jnp.sin(angle)
-    rest = jnp.zeros((rows, HEAD_DIM - ROT_DIM), F32)
-    none = jnp.zeros_like(sine)
+    lane = jnp.arange(PAIR, dtype=jnp.int32) % HEAD_DIM
+    inverse = rotary_base ** (-((lane % half).astype(F32) * 2.0 / ROT_DIM))
+    angle = position[:, None] * jnp.where(lane < ROT_DIM, inverse, 0.0)[None, :]
+    sine = jnp.sin(angle)
     rope = jnp.stack(
-        [
-            jnp.tile(jnp.concatenate([cosine, cosine, rest + 1.0], axis=1), (1, 2)),
-            jnp.tile(jnp.concatenate([-sine, none, rest], axis=1), (1, 2)),
-            jnp.tile(jnp.concatenate([none, sine, rest], axis=1), (1, 2)),
-        ]
+        [jnp.cos(angle), jnp.where(lane < half, -sine, 0.0), jnp.where((lane >= half) & (lane < ROT_DIM), sine, 0.0)]
     )
-    allowed = (segment_ids[:, None] == segment_ids[None, :]) & (places[None, :] <= places[:, None])
-    return rope, jnp.where(allowed, 0.0, -1e30)
+    return rope, jnp.where(same & (places[None, :] <= places[:, None]), 0.0, -1e30)
 
 
 def on_device(

time: 730 us -> 727 us (level)
  no operation moved by 1% of the time
where the time goes in v3:
time: 727 us; the launch traced here: 725 us
  Pallas kernels  708 us (97%)
  local copies, waits for them, and re-layouts  12 us (2%)
    pallas_call x1, Pallas kernels, train(): pl.pallas_call(functools.partial(train_kernel, count, shards, steps, span...  692 us
    pallas_call x1, Pallas kernels, finish(): pl.pallas_call(finish_kernel, grid=(LAYERS, cuts), in_specs=[spec((1, par...  15.4 us

profile of v3, /device:TPU:17, one launch (start us, length us, event | category | flops | bytes accessed | tf_op | source)
XLA Modules:
  0.0 725.5 jit_solution(11497556653752035282)
XLA Ops:
  0.7 1.1 select_reduce_fusion
  1.7 1.1 multiply_cosine_fusion
  2.9 1.0 pad_maximum_fusion.rope
  3.9 0.0 copy-start.1
  3.9 3.8 copy.54
  7.7 0.0 copy-start.4
  7.7 0.0 copy-start.2
  7.7 0.0 copy-done.1
  7.7 0.0 copy-start.7
  7.7 0.0 copy-start.8
  7.7 0.0 copy-start.9
  7.7 0.0 copy-start.10
  7.8 0.0 copy-start.6
  7.8 1.5 copy.44
  9.3 0.0 copy-done.4
  9.3 0.1 eq.29
  9.4 1.2 select_convert_fusion.mask
  10.6 0.0 copy-done.2
  10.6 1.0 copy.42
  11.6 0.0 copy-done.7
  11.6 0.0 copy-done.8
  11.7 0.0 copy-done.9
  11.7 0.0 copy-done.10
  11.7 0.6 reshape.256.own_norms
  12.3 0.0 copy-done.6
  12.3 0.1 convert_element_type.23
  12.4 0.6 pad_convert_fusion.own_bias
  13.0 692.2 %train.1 = (bf16[576,2048]{1,0:T(8,128)(2,1)}, f32[576,2048]{1,0:T(8,128)}, bf16[2,3,256,2048]{3,2,1,0:T(8,128)(2,1)}, bf16[2,3,256,4224]{3,2,1,0:T(8,128)(2,1)}...) custom-call(bf16[576,2048]{1,0:T(8,128)(2,1)} %states.1, ...), custom_call_target="tpu_custom_call" | custom-call | flops 88785027072 | bytes 346816512 | tf_op jit(solution)/shard_map/train/pallas_call | solution.py:1125
  705.2 0.0 copy-start
  705.2 1.7 copy-done
  706.9 0.0 copy-start.3
  706.9 0.0 copy-start.5
  706.9 15.4 %finish.1 = (f32[2,3,256,512]{3,2,1,0:T(8,128)}, f32[2,512,256]{2,1,0:T(8,128)}, f32[2,256,2,1408]{3,2,1,0:T(2,128)}, f32[2,1408,256]{2,1,0:T(8,128)}, bf16[576,2048]{1,0:T(8,128)(2,1)}, /*index=5*/f32[576,2048]{1,0:T(8,128)}) custom-call(bf16[2,3,256,2048]{3,2,1,0:T(8,128)(2,1)} %get-tuple-element.23.attn, bf16[2,3,256,4224]{3,2,1,0:T(8,128)(2,1)} %get-tuple-element.24.ffn, ...), custom_call_target="tpu_custom_call" | custom-call | tf_op jit(solution)/shard_map/finish/pallas_call | solution.py:1164
  722.3 0.0 copy-done.3
  722.4 0.1 reshape.255
  722.4 0.7 constant_dynamic-slice_fusion
  723.1 0.0 copy-done.5
  723.2 0.6 copy.55
  723.7 0.6 copy.56
  724.3 0.6 copy.57
  724.9 0.6 copy.58
  (13 shorter events, 0.1 us)
Async XLA Ops:
  3.9 3.9 copy-start.1
  7.7 1.6 copy-start.4
  7.7 2.9 copy-start.2
  7.7 3.9 copy-start.7
  7.7 3.9 copy-start.8
  7.7 3.9 copy-start.9
  7.7 3.9 copy-start.10
  7.8 4.6 copy-start.6
  705.2 1.7 copy-start
  706.9 15.4 %copy-start.3 = (f32[8,2,8,512]{3,2,1,0:T(8,128)S(1)}, f32[8,2,8,512]{3,2,1,0:T(8,128)}, u32[]{:S(2)}) copy-start(f32[8,2,8,512]{3,2,1,0:T(8,128)} %get-tuple-element.31) | copy-start | bytes 786436
  706.9 16.2 %copy-start.5 = (f32[8,8,256]{2,1,0:T(8,128)S(1)}, f32[8,8,256]{2,1,0:T(8,128)}, u32[]{:S(2)}) copy-start(f32[8,8,256]{2,1,0:T(8,128)} %get-tuple-element.29) | copy-start | bytes 196612

commit v4 on v3

--- a/solution.py
+++ b/solution.py
@@ -670,15 +670,23 @@
             else:
                 self.right = [(0, qkv.at[0]), (0, qkv.at[1]), (0, qkv.at[2]), (1, att)]
 
+        def own(self, u):
+            return (u == 3) | (u >= 5) if group.square else u >= chips
+
+        def place(self, u):
+            if not group.square:
+                return u % chips
+            return jnp.where(u < 3, u, jnp.where(u == 3, 0, jnp.where(u == 4, 3, u - 4)))
+
         def chip(self, u):
             if not group.square:
                 return (group.chip + 1 + u) % chips
             x, y, far = group.x // 2, group.y // 2, group.far // 2
-            k = u % 4
+            k = self.place(u)
             return jnp.where(k == 0, far, jnp.where(k == 1, x, jnp.where(k == 2, y, group.chip)))
 
         def fetch(self, u):
-            core = jnp.where(u < chips, 1 - group.core, group.core)
+            core = jnp.where(self.own(u), group.core, 1 - group.core)
             at = pl.multiple_of((self.chip(u) * 2 + core) * depth, depth)
             return [
                 pltpu.make_async_copy(
@@ -730,7 +738,7 @@
                 return
             for k, hops in enumerate(((0, 1), (2,), (3,))):
 
-                @when(u % 4 == k)
+                @when(self.place(u) == k)
                 def _(hops=hops):
                     for kind in hops:
                         start(*self.hop(kind))
@@ -769,24 +777,24 @@
 
         def unit(self, u):
             slot = u % 2
-            own = u >= chips
+            own = self.own(u)
 
             @when(u + 1 < units)
             def _():
                 for copy in self.fetch(u + 1):
                     copy.start()
 
-            @when((u >= 2) & (u < chips + 2))
+            @when((u >= 2) & jnp.logical_not(self.own(u - 2)))
             def _():
                 whole(*self.over(u - 2)).wait_send()
 
-            @when(u > chips)
+            @when((u >= 1) & self.own(u - 1))
             def _():
                 self.send_on(u - 1)
 
             @when(own)
             def _():
-                whole(*self.over(u - chips)).wait_recv()
+                whole(*self.over(u)).wait_recv()
                 start(*self.bring(u))
 
             for copy in self.fetch(u):
@@ -982,8 +990,10 @@
             def _(k=k):
                 blocks = Blocks(back - 1, k)
                 extra = back == half
-                pace = jnp.where(extra, 2 * per_step, per_step)
-                blocks.run(jnp.minimum(i * pace, units), jnp.minimum((i + 1) * pace, units))
+                pace = 2 * per_step
+                first = jnp.where(extra, jnp.minimum(i * pace, units), i * units // steps)
+                last = jnp.where(extra, jnp.minimum((i + 1) * pace, units), (i + 1) * units // steps)
+                blocks.run(first, last)
 
                 @when(i == jnp.where(extra, min(3, steps - 1), steps - 1))
                 def _():

time: 727 us -> 733 us (level)
  no operation moved by 1% of the time
where the time goes in v4:
time: 733 us; the launch traced here: 732 us
  Pallas kernels  714 us (97%)
  local copies, waits for them, and re-layouts  12 us (2%)
    pallas_call x1, Pallas kernels, train(): pl.pallas_call(functools.partial(train_kernel, count, shards, steps, span...  699 us
    pallas_call x1, Pallas kernels, finish(): pl.pallas_call(finish_kernel, grid=(LAYERS, cuts), in_specs=[spec((1, par...  15.4 us

profile of v4, /device:TPU:17, one launch (start us, length us, event | category | flops | bytes accessed | tf_op | source)
XLA Modules:
  0.0 732.1 jit_solution(5547228617864902668)
XLA Ops:
  0.7 1.1 select_reduce_fusion
  1.7 1.1 multiply_cosine_fusion
  2.9 1.0 pad_maximum_fusion.rope
  3.9 0.0 copy-start.1
  3.9 3.8 copy.54
  7.7 0.0 copy-start.4
  7.7 0.0 copy-start.2
  7.7 0.0 copy-done.1
  7.7 0.0 copy-start.7
  7.7 0.0 copy-start.8
  7.7 0.0 copy-start.9
  7.7 0.0 copy-start.10
  7.8 0.0 copy-start.6
  7.8 1.5 copy.44
  9.3 0.0 copy-done.4
  9.3 0.1 eq.29
  9.4 1.2 select_convert_fusion.mask
  10.6 0.0 copy-done.2
  10.6 1.0 copy.42
  11.6 0.0 copy-done.7
  11.6 0.0 copy-done.8
  11.7 0.0 copy-done.9
  11.7 0.0 copy-done.10
  11.7 0.6 reshape.256.own_norms
  12.3 0.0 copy-done.6
  12.3 0.1 convert_element_type.23
  12.4 0.6 pad_convert_fusion.own_bias
  13.0 698.8 %train.1 = (bf16[576,2048]{1,0:T(8,128)(2,1)}, f32[576,2048]{1,0:T(8,128)}, bf16[2,3,256,2048]{3,2,1,0:T(8,128)(2,1)}, bf16[2,3,256,4224]{3,2,1,0:T(8,128)(2,1)}...) custom-call(bf16[576,2048]{1,0:T(8,128)(2,1)} %states.1, ...), custom_call_target="tpu_custom_call" | custom-call | flops 88785027072 | bytes 346816512 | tf_op jit(solution)/shard_map/train/pallas_call | solution.py:1135
  711.8 0.0 copy-start
  711.8 1.7 copy-done
  713.5 0.0 copy-start.3
  713.5 0.0 copy-start.5
  713.5 15.4 %finish.1 = (f32[2,3,256,512]{3,2,1,0:T(8,128)}, f32[2,512,256]{2,1,0:T(8,128)}, f32[2,256,2,1408]{3,2,1,0:T(2,128)}, f32[2,1408,256]{2,1,0:T(8,128)}, bf16[576,2048]{1,0:T(8,128)(2,1)}, /*index=5*/f32[576,2048]{1,0:T(8,128)}) custom-call(bf16[2,3,256,2048]{3,2,1,0:T(8,128)(2,1)} %get-tuple-element.23.attn, bf16[2,3,256,4224]{3,2,1,0:T(8,128)(2,1)} %get-tuple-element.24.ffn, ...), custom_call_target="tpu_custom_call" | custom-call | tf_op jit(solution)/shard_map/finish/pallas_call | solution.py:1174
  728.9 0.0 copy-done.3
  729.0 0.1 reshape.255
  729.0 0.7 constant_dynamic-slice_fusion
  729.7 0.0 copy-done.5
  729.8 0.6 copy.55
  730.4 0.6 copy.56
  730.9 0.6 copy.57
  731.5 0.6 copy.58
  (13 shorter events, 0.1 us)
Async XLA Ops:
  3.9 3.9 copy-start.1
  7.7 1.6 copy-start.4
  7.7 2.9 copy-start.2
  7.7 3.9 copy-start.7
  7.7 3.9 copy-start.8
  7.7 3.9 copy-start.9
  7.7 3.9 copy-start.10
  7.8 4.6 copy-start.6
  711.8 1.7 copy-start
  713.5 15.4 %copy-start.3 = (f32[8,2,8,512]{3,2,1,0:T(8,128)S(1)}, f32[8,2,8,512]{3,2,1,0:T(8,128)}, u32[]{:S(2)}) copy-start(f32[8,2,8,512]{3,2,1,0:T(8,128)} %get-tuple-element.31) | copy-start | bytes 786436
  713.5 16.2 %copy-start.5 = (f32[8,8,256]{2,1,0:T(8,128)S(1)}, f32[8,8,256]{2,1,0:T(8,128)}, u32[]{:S(2)}) copy-start(f32[8,8,256]{2,1,0:T(8,128)} %get-tuple-element.29) | copy-start | bytes 196612
